TPU v7x, 128 devices: a whole 4x4x4 slice. The times are simulated.
128 devices in a mesh: row: 16 (over y_hi, x, core), col: 8 (over y_lo, z).
Axes of the slice: x: 4, y: 4 (y_hi: 2, y_lo: 2; y = y_hi * 2 + y_lo), z: 4, core: 2. Of those that a mesh axis runs over, the one named last changes fastest.
Arguments:
- pair: float32 [512, 512, 128], P('row', 'col'), may hold values from -6 to 6
- token_mask: int32 [512], replicated, may hold values 0 or 1
- out_proj: float32 [128, 640], replicated, may hold values from -0.5 to 0.5
- out_final: float32 [128, 128], replicated, may hold values from -0.5 to 0.5
- in_proj: float32 [128, 640], replicated, may hold values from -0.5 to 0.5
- in_final: float32 [128, 128], replicated, may hold values from -0.5 to 0.5
Outputs:
- updated: float32 [512, 512, 128], P('row', 'col')
All inputs are finite; a program needn't handle non-finite values.
Results may differ from a plain program's by a relative error of at most 0.0065.
Values may be sent and summed in bfloat16 or wider, within the bound.
No kernel may reach another device: no remote copies, remote signals or barrier semaphores. Data moves between devices by JAX's collectives and lax.ppermute only.
A program may use at most 128 MiB of HBM per device.

v0:
```python
import jax
import jax.numpy as jnp
from jax import lax
from jax.sharding import PartitionSpec as P


def layer_norm(values):
    centred = values - jnp.mean(values, axis=-1, keepdims=True)
    variance = jnp.mean(centred * centred, axis=-1, keepdims=True)
    return centred * lax.rsqrt(variance + 1e-05)


def project(pair, pair_mask, weights, hidden):
    linear = jnp.einsum("ijd,de->ije", layer_norm(pair), weights, precision=lax.Precision.HIGHEST)
    left_side = (
        jax.nn.sigmoid(linear[..., hidden : 2 * hidden])
        * linear[..., :hidden]
        * pair_mask[..., None]
    )
    right_side = (
        jax.nn.sigmoid(linear[..., 3 * hidden : 4 * hidden])
        * linear[..., 2 * hidden : 3 * hidden]
        * pair_mask[..., None]
    )
    gating = jax.nn.sigmoid(linear[..., 4 * hidden :])
    return (left_side.astype(jnp.bfloat16), right_side.astype(jnp.bfloat16), gating)


def finish(pair, gating, triangle, final):
    return pair + gating * jnp.einsum(
        "ijh,hd->ijd", layer_norm(triangle), final, precision=lax.Precision.HIGHEST
    )


def shards(pair, token_mask, out_proj, out_final, in_proj, in_final):
    row_count, col_count, channels = pair.shape
    hidden = out_final.shape[0]
    row_pos = lax.axis_index("row")
    col_pos = lax.axis_index("col")
    row_mask = lax.dynamic_slice_in_dim(token_mask, row_pos * row_count, row_count).astype(
        jnp.float32
    )
    col_mask = lax.dynamic_slice_in_dim(token_mask, col_pos * col_count, col_count).astype(
        jnp.float32
    )
    pair_mask = row_mask[:, None] * col_mask[None, :]
    left_side, right_side, gating = project(pair, pair_mask, out_proj, hidden)
    partial_sums = jnp.einsum(
        "ikc,jkc->ijc",
        left_side,
        lax.all_gather(right_side, "row", axis=0, tiled=True),
        preferred_element_type=jnp.float32,
    )
    triangle = lax.psum_scatter(partial_sums, "col", scatter_dimension=1, tiled=True)
    first = finish(pair, gating, triangle, out_final)
    left_side, right_side, gating = project(first, pair_mask, in_proj, hidden)
    partial_sums = jnp.einsum(
        "kic,kjc->ijc",
        lax.all_gather(left_side, "col", axis=1, tiled=True),
        right_side,
        preferred_element_type=jnp.float32,
    )
    triangle = lax.psum_scatter(
        partial_sums.astype(jnp.bfloat16), "row", scatter_dimension=0, tiled=True
    ).astype(jnp.float32)
    return finish(first, gating, triangle, in_final)


def solution(mesh):
    placed = (P("row", "col", None), P(), P(), P(), P(), P())
    return jax.shard_map(
        shards, mesh=mesh, in_specs=placed, out_specs=P("row", "col", None), check_vma=False
    )
```

profile of v0, /device:TPU:1, one launch (start us, length us, event | category | flops | bytes accessed | tf_op | source)
XLA Modules:
  0.0 446.4 jit_solution(7948577478691770699)
XLA Ops:
  6.5 0.0 copy-start
  6.5 0.0 all-gather.3.cloned.1.call-start
  6.5 0.8 dynamic-slice_convert_fusion
  7.3 0.8 dynamic-slice_convert_fusion.1
  8.1 1.6 reduce_sum.72
  9.7 1.9 multiply_reduce_fusion.2
  11.6 0.1 broadcast_multiply_fusion
  11.6 0.0 copy-done
  11.6 5.9 %fusion.35 = f32[32,64,640]{2,1,0:T(8,128)S(1)} fusion(f32[32,64,128]{2,1,0:T(8,128)} %param.6, f32[32,64]{1,0:T(8,128)S(1)} %add_rsqrt_fusion.3, f32[32,64]{1,0:T(8,128)S(1)} %broadcast_multiply_fusion.4, f32[128,640]{1,0:T(8,128)S(1)} %copy-done), kind=kOutput, calls=%fused_computation.52 | convolution fusion | flops 2013790208 | bytes 6635520 | tf_op jit(solution)/shard_map/ijd,de->ije/dot_general | solution.py:14
  17.5 0.0 copy-start.2
  17.5 2.4 copy-done.2
  19.9 1.4 fusion.20
  21.3 0.0 all-gather.3.cloned.1.call-update
  21.3 0.0 reduce-scatter.3.cloned.1.call-start
  21.4 1.6 copy.44
  23.0 74.8 %all-gather.3.cloned.1.call-done = bf16[512,64,128]{2,1,0:T(8,128)(2,1)} async-done(((bf16[32,64,128]{2,1,0:T(8,128)(2,1)}), bf16[512,64,128]{2,1,0:T(8,128)(2,1)}) %all-gather.3.cloned.1.call-update) | async-done | bytes 8388624 | tf_op jit(solution)/shard_map/all_gather | solution.py:51
  97.8 23.7 %copy.43 = bf16[512,64,128]{1,0,2:T(8,128)(2,1)} copy(bf16[512,64,128]{2,1,0:T(8,128)(2,1)} %all-gather.3.cloned.1.call-done) | data formatting | bytes 16777216 | tf_op jit(solution)/shard_map/all_gather | solution.py:51
  121.5 11.3 %convolution_bitcast_fusion = f32[32,512,128]{1,0,2:T(8,128)} fusion(bf16[512,64,128]{1,0,2:T(8,128)(2,1)} %copy.43, bf16[32,64,128]{1,0,2:T(8,128)(2,1)S(1)} %copy.44), kind=kOutput, calls=%fused_computation.1 | convolution fusion | flops 268435456 | bytes 17301504 | tf_op jit(solution)/shard_map/ikc,jkc->ijc/dot_general | solution.py:48
  132.8 11.0 %copy.45 = f32[32,512,128]{2,0,1:T(8,128)} copy(f32[32,512,128]{1,0,2:T(8,128)} %convolution_bitcast_fusion) | data formatting | bytes 16777216 | tf_op jit(solution)/shard_map/ikc,jkc->ijc/transpose | solution.py:48
  143.8 0.0 copy-start.4
  143.8 0.0 copy-start.6
  143.8 0.0 reduce-scatter.3.cloned.1.call-update
  143.8 0.2 all-gather.5.cloned.1.call-start
  144.1 90.3 %reduce-scatter.3.cloned.1.call-done = f32[32,64,128]{2,0,1:T(8,128)} async-done(((f32[32,512,128]{2,0,1:T(8,128)}), f32[32,64,128]{2,0,1:T(8,128)}) %reduce-scatter.3.cloned.1.call-update) | async-done | bytes 1048592 | tf_op jit(solution)/shard_map/reduce_scatter | solution.py:54
  234.4 1.6 reduce_sum.74
  235.9 0.0 copy-start.5
  235.9 0.1 copy.46
  236.0 0.1 copy.47
  236.1 1.9 multiply_reduce_fusion.1
  238.0 0.1 copy.48
  238.1 0.1 copy.49
  238.1 1.8 subtract_multiply_fusion
  240.0 0.0 copy-done.4
  240.0 0.0 copy-done.6
  240.0 3.0 fusion.49
  243.1 0.6 multiply_reduce_fusion
  243.7 0.0 copy-done.5
  243.7 4.6 %fusion.33 = f32[32,64,640]{2,1,0:T(8,128)S(1)} fusion(f32[32,64,128]{2,1,0:T(8,128)S(1)} %get-tuple-element.10, f32[32,64]{1,0:T(8,128)S(1)} %add_rsqrt_fusion.1, f32[32,64]{1,0:T(8,128)S(1)} %broadcast_multiply_fusion.2, f32[128,640]{1,0:T(8,128)S(1)} %copy-done.5), kind=kOutput, calls=%fused_computation.48 | convolution fusion | flops 2013790208 | bytes 6635520 | tf_op jit(solution)/shard_map/ijd,de->ije/dot_general | solution.py:14
  248.4 0.0 copy-start.3
  248.4 2.3 copy-done.3
  250.7 1.4 fusion.7
  252.1 0.0 all-gather.5.cloned.1.call-update
  252.1 0.3 reduce-scatter.5.cloned.1.call-start
  252.4 1.6 copy.51
  254.0 49.7 %all-gather.5.cloned.1.call-done = bf16[32,512,128]{2,1,0:T(8,128)(2,1)} async-done(((bf16[32,64,128]{2,1,0:T(8,128)(2,1)}), bf16[32,512,128]{2,1,0:T(8,128)(2,1)}) %all-gather.5.cloned.1.call-update) | async-done | bytes 4194320 | tf_op jit(solution)/shard_map/all_gather | solution.py:59
  303.7 7.9 %copy.52 = bf16[32,512,128]{1,0,2:T(8,128)(2,1)} copy(bf16[32,512,128]{2,1,0:T(8,128)(2,1)} %all-gather.5.cloned.1.call-done) | data formatting | bytes 8388608 | tf_op jit(solution)/shard_map/all_gather | solution.py:59
  311.6 7.8 %convert_bitcast_fusion = bf16[512,64,128]{0,1,2:T(8,128)(2,1)} fusion(bf16[32,64,128]{1,0,2:T(8,128)(2,1)S(1)} %copy.51, bf16[32,512,128]{1,0,2:T(8,128)(2,1)} %copy.52), kind=kOutput, calls=%fused_computation | convolution fusion | flops 272629760 | bytes 13107200 | tf_op jit(solution)/shard_map/kic,kjc->ijc/dot_general | solution.py:57
  319.4 13.7 %copy.53 = bf16[512,64,128]{2,1,0:T(8,128)(2,1)} copy(bf16[512,64,128]{0,1,2:T(8,128)(2,1)} %convert_bitcast_fusion) | data formatting | bytes 16777216 | tf_op jit(solution)/shard_map/convert_element_type | solution.py:64
  333.0 0.0 copy-start.7
  333.1 0.0 reduce-scatter.5.cloned.1.call-update
  333.1 0.0 copy-start.1
  333.1 100.0 %reduce-scatter.5.cloned.1.call-done = bf16[32,64,128]{2,1,0:T(8,128)(2,1)} async-done(((bf16[512,64,128]{2,1,0:T(8,128)(2,1)}), bf16[32,64,128]{2,1,0:T(8,128)(2,1)}) %reduce-scatter.5.cloned.1.call-update) | async-done | bytes 524304 | tf_op jit(solution)/shard_map/reduce_scatter | solution.py:63
  433.1 1.4 convert_reduce_fusion
  434.5 1.7 fusion.4
  436.2 0.0 copy-done.7
  436.2 3.7 fusion
  439.9 0.0 copy-done.1
  (8 shorter events, 0.1 us)
Async XLA Ops:
  6.5 5.1 %copy-start = (f32[128,640]{1,0:T(8,128)S(1)}, f32[128,640]{1,0:T(8,128)}, u32[]{:S(2)}) copy-start(f32[128,640]{1,0:T(8,128)} %param.8) | copy-start | bytes 983044
  6.5 91.2 %all-gather.3.cloned.1.call-start = ((), (), s32[]{:S(2)}) async-start(), calls=%async_computation.2 | async-start | bytes 8912896 | tf_op jit(solution)/shard_map/all_gather | solution.py:51
  17.5 2.4 copy-start.2
  21.3 213.1 %reduce-scatter.3.cloned.1.call-start = ((), (), s32[]{:S(2)}) async-start(), calls=%async_computation.3 | async-start | bytes 9437184 | tf_op jit(solution)/shard_map/reduce_scatter | solution.py:54
  143.8 96.2 %copy-start.4 = (f32[32,64,128]{2,1,0:T(8,128)S(1)}, f32[32,64,128]{2,1,0:T(8,128)}, u32[]{:S(2)}) copy-start(f32[32,64,128]{2,1,0:T(8,128)} %param.6) | copy-start | bytes 3145732
  143.8 96.2 %copy-start.6 = (f32[128,128]{1,0:T(8,128)S(1)}, f32[128,128]{1,0:T(8,128)}, u32[]{:S(2)}) copy-start(f32[128,128]{1,0:T(8,128)} %param.9) | copy-start | bytes 196612
  143.8 159.9 %all-gather.5.cloned.1.call-start = ((), (), s32[]{:S(2)}) async-start(), calls=%async_computation.4 | async-start | bytes 4718592 | tf_op jit(solution)/shard_map/all_gather | solution.py:59
  235.9 7.8 %copy-start.5 = (f32[128,640]{1,0:T(8,128)S(1)}, f32[128,640]{1,0:T(8,128)}, u32[]{:S(2)}) copy-start(f32[128,640]{1,0:T(8,128)} %param.10) | copy-start | bytes 983044
  248.4 2.3 copy-start.3
  252.1 181.0 %reduce-scatter.5.cloned.1.call-start = ((), (), s32[]{:S(2)}) async-start(), calls=%async_computation.5 | async-start | bytes 8912896 | tf_op jit(solution)/shard_map/reduce_scatter | solution.py:63
  333.0 103.2 %copy-start.7 = (f32[128,128]{1,0:T(8,128)S(1)}, f32[128,128]{1,0:T(8,128)}, u32[]{:S(2)}) copy-start(f32[128,128]{1,0:T(8,128)} %param.11) | copy-start | bytes 196612
  333.1 106.8 %copy-start.1 = (f32[128,640]{1,0:T(8,128)S(1)}, f32[128,640]{1,0:T(8,128)}, u32[]{:S(2)}) copy-start(f32[128,640]{1,0:T(8,128)} %param.8) | copy-start | bytes 983044
Sparse Core Ops, SparseCore 0:
  21.4 76.3 all-gather.2
  143.9 90.3 reduce-scatter.2
  252.2 51.4 all-gather.4
  333.2 99.8 reduce-scatter.4
where the time goes:
time: 449 us; the launch traced here: 446 us
  waiting for transfers between devices  315 us (70%)
  local copies, waits for them, and re-layouts  64.5 us (14%)
  matrix products  36.3 us (8%)
  other arithmetic  16.9 us (4%)
  between operations  13.3 us (3%)
    reduce_scatter x1, waiting for transfers between devices, shards(): lax.psum_scatter(partial_sums.astype(jnp.bfloat16), 'row', scatter_dimens...  100 us
    reduce_scatter x1, waiting for transfers between devices, shards(): lax.psum_scatter(partial_sums, 'col', scatter_dimension=1, tiled=True)  90.3 us
    all_gather x1, waiting for transfers between devices, shards(): lax.all_gather(right_side, 'row', axis=0, tiled=True)  74.8 us
    all_gather x1, waiting for transfers between devices, shards(): lax.all_gather(left_side, 'col', axis=1, tiled=True)  49.7 us
    all_gather x1, local copies, waits for them, and re-layouts, shards(): lax.all_gather(right_side, 'row', axis=0, tiled=True)  23.7 us
    convert_element_type x1, local copies, waits for them, and re-layouts, shards(): partial_sums.astype(jnp.bfloat16)  13.7 us
    dot_general x1, matrix products, shards(): jnp.einsum('ikc,jkc->ijc', left_side, lax.all_gather(right_side, 'row', a...  11.3 us
    transpose x1, local copies, waits for them, and re-layouts, shards(): jnp.einsum('ikc,jkc->ijc', left_side, lax.all_gather(right_side, 'row', a...  11 us
  transfers between devices with their start and end apart: 4, of which 4 were waited for; matrix products, arithmetic and copies ran while one was open for 1% of the time, Pallas kernels for 0%

commit v1 on v0

v1 whole, which is shorter than its diff:
```python
import functools

import jax
import jax.numpy as jnp
from jax import lax
from jax.experimental import pallas as pl
from jax.experimental.pallas import tpu as pltpu
from jax.sharding import PartitionSpec as P

HALF = 64
TILES = 16
F32 = jnp.float32
BF16 = jnp.bfloat16
VMEM = pl.BlockSpec(memory_space=pltpu.VMEM)
SMEM = pl.BlockSpec(memory_space=pltpu.SMEM)


def call(kernel, outs, scratch, specs, flops):
    return pl.pallas_call(
        kernel,
        out_shape=outs,
        in_specs=specs,
        out_specs=jax.tree.map(lambda _: VMEM, outs),
        scratch_shapes=scratch,
        compiler_params=pltpu.CompilerParams(vmem_limit_bytes=48 * 1024 * 1024),
        cost_estimate=pl.CostEstimate(flops=flops, bytes_accessed=3 << 20, transcendentals=1 << 19),
    )


def low_lanes(shape):
    return lax.broadcasted_iota(jnp.int32, shape, len(shape) - 1) < HALF


def turn(values):
    return pltpu.roll(values, HALF, axis=values.ndim - 1)


def gate(values):
    return 0.5 * jnp.tanh(0.5 * values) + 0.5


def norm(values):
    scale = 1.0 / values.shape[0]
    centred = values - jnp.sum(values, axis=0, keepdims=True) * scale
    variance = jnp.sum(centred * centred, axis=0, keepdims=True) * scale
    return centred * lax.rsqrt(variance + 1e-05)


def dot(left, right, dims=((1,), (0,))):
    return lax.dot_general(left, right, (dims, ((), ())), preferred_element_type=F32)


def transposed(weights, start, stop):
    parts = [weights[:, k : k + 128].T for k in range(start, stop, 128)]
    return jnp.concatenate(parts, axis=0).astype(BF16)


def masks(token_s, token_v):
    row = lax.axis_index("row")
    col = lax.axis_index("col")
    line = token_v[pl.ds(col // 2, 1), :].astype(F32)
    low = low_lanes((1, 128))
    odd = col % 2
    pick = jnp.where(low, 1, 0) != odd
    cols = jnp.where(pick, line, turn(line))

    def of_tile(tile):
        first = row * 32 + (tile // 8) * 16 + tile % 8
        top = token_s[first].astype(F32)
        bottom = token_s[first + 8].astype(F32)
        return cols * jnp.where(low, top, bottom)

    return of_tile


def pair_tile(pair, tile):
    first = (tile // 8) * 16 + tile % 8
    return jnp.concatenate([pair[first], pair[first + 8]], axis=0).T


def sides(normed, weights, mask, low, held, slot):
    linear = dot(weights, normed)
    left = gate(linear[128:256]) * linear[0:128] * mask
    right = gate(linear[384:512]) * linear[256:384] * mask
    for k in range(2):
        lanes = slice(128 * k, 128 * (k + 1))
        held[slot + k] = jnp.where(low, left[:, lanes], turn(right[:, lanes]))
        held[slot + k + 8] = jnp.where(low, turn(left[:, lanes]), right[:, lanes])


def pack(held, out, group):
    for k in range(0, 128, 32):
        out[k : k + 32, 16 * group : 16 * group + 16, :] = jnp.swapaxes(held[:, k : k + 32, :], 0, 1).astype(BF16)


def project_kernel(token_s, token_v, pair, proj, out, held):
    weights = transposed(proj, 0, 512)
    of_tile = masks(token_s, token_v)
    low = low_lanes((128, 128))
    for group in range(2):
        for slot in range(0, 8, 2):
            tile = 8 * group + slot
            mask = jnp.concatenate([of_tile(tile), of_tile(tile + 1)], axis=1)
            values = jnp.concatenate([pair_tile(pair, tile), pair_tile(pair, tile + 1)], axis=1)
            sides(norm(values).astype(BF16), weights, mask, low, held, slot)
        pack(held, out, group)


def gating_kernel(pair, proj, flat, gating):
    weights = transposed(proj, 512, 640)
    for tile in range(0, TILES, 2):
        values = jnp.concatenate([pair_tile(pair, tile), pair_tile(pair, tile + 1)], axis=1)
        lanes = slice(128 * tile, 128 * (tile + 2))
        flat[:, lanes] = values
        gating[:, lanes] = gate(dot(weights, norm(values).astype(BF16)))


def operands(got, left, right):
    for k in range(4):
        lanes = slice(128 * k, 128 * (k + 1))
        even = got[:, 2 * k].reshape(512, 128)
        odd = got[:, 2 * k + 1].reshape(512, 128)
        left[:, lanes] = jnp.concatenate([even[:, :HALF], odd[:, :HALF]], axis=1)
        right[:, lanes] = jnp.concatenate([even[:, HALF:], odd[:, HALF:]], axis=1)


def triangle_kernel(contract, got, out, left, right):
    operands(got, left, right)
    low = low_lanes((16, 128))
    for k in range(0, 16, 4):
        rows = slice(32 * k, 32 * (k + 4))
        if contract == 1:
            sums = dot(left[rows, :], right[...], ((1,), (1,)))
        else:
            sums = dot(left[:, rows], right[...], ((0,), (0,)))
        sums = sums.reshape(4, 2, 2, 8, 512)
        for n in range(4):
            for m in range(4):
                lanes = slice(128 * m, 128 * (m + 1))
                top = sums[n, :, 0, :, lanes].reshape(16, 128)
                bottom = sums[n, :, 1, :, lanes].reshape(16, 128)
                out[k + n, 2 * m] = jnp.where(low, top, turn(bottom)).astype(BF16)
                out[k + n, 2 * m + 1] = jnp.where(low, turn(top), bottom).astype(BF16)


def unpack(got, held):
    for k in range(0, 128, 32):
        held[:, k : k + 32, :] = jnp.swapaxes(got[k : k + 32].astype(F32), 0, 1)


def middle_kernel(token_s, token_v, got, flat, gating, final, proj, out, first, held, triangle):
    weights = transposed(proj, 0, 512)
    closing = transposed(final, 0, 128)
    of_tile = masks(token_s, token_v)
    low = low_lanes((128, 128))
    unpack(got, triangle)
    for group in range(2):
        for slot in range(0, 8, 2):
            tile = 8 * group + slot
            lanes = slice(128 * tile, 128 * (tile + 2))
            mask = jnp.concatenate([of_tile(tile), of_tile(tile + 1)], axis=1)
            values = norm(jnp.concatenate([triangle[tile], triangle[tile + 1]], axis=1)).astype(BF16)
            values = flat[:, lanes] + gating[:, lanes] * dot(closing, values)
            first[:, lanes] = values
            sides(norm(values).astype(BF16), weights, mask, low, held, slot)
        pack(held, out, group)


def second_gating_kernel(first, proj, turned, gating):
    weights = proj[:, 512:640].astype(BF16)
    for tile in range(TILES):
        values = first[:, 128 * tile : 128 * (tile + 1)]
        turned[tile] = values.T
        gating[tile] = gate(dot(norm(values).astype(BF16), weights, ((0,), (0,))))


def last_kernel(got, turned, gating, final, out, triangle):
    closing = final[...].astype(BF16)
    unpack(got, triangle)
    for tile in range(TILES):
        row = (tile // 8) * 16 + tile % 8
        values = turned[tile] + gating[tile] * dot(norm(triangle[tile]).astype(BF16), closing, ((0,), (0,)))
        out[row] = values[:HALF]
        out[row + 8] = values[HALF:]


def shards(pair, token_mask, out_proj, out_final, in_proj, in_final):
    axes = ("row", "col")
    struct = jax.ShapeDtypeStruct
    lines = token_mask.reshape(4, 128)
    message = struct((128, 32, 128), BF16)
    answer = struct((16, 8, 16, 128), BF16)
    whole = struct((128, 2048), F32)
    held = pltpu.VMEM((16, 128, 128), F32)
    operand = pltpu.VMEM((512, 512), BF16)

    def swap(values):
        return lax.all_to_all(values, axes, 0, 0, tiled=True)

    def triangle(got, contract):
        kernel = functools.partial(triangle_kernel, contract)
        sums = call(kernel, answer, [operand, operand], [VMEM], 2 * 512**3)(got.reshape(16, 8, 32, 128))
        return sums.reshape(128, 16, 128)

    sent = call(project_kernel, message, [held], [SMEM, VMEM, VMEM, VMEM], 2 * 2048 * 128 * 512)(
        token_mask, lines, pair, out_proj
    )
    flat, gating = call(gating_kernel, (whole, whole), [], [VMEM, VMEM], 2 * 2048 * 128 * 128)(pair, out_proj)
    sums = swap(triangle(swap(sent), 1))
    sent, first = call(
        middle_kernel, (message, whole), [held, held], [SMEM] + [VMEM] * 6, 2 * 2048 * 128 * 640
    )(token_mask, lines, sums, flat, gating, out_final, in_proj)
    tiles = struct((TILES, 128, 128), F32)
    turned, gating = call(second_gating_kernel, (tiles, tiles), [], [VMEM, VMEM], 2 * 2048 * 128 * 128)(first, in_proj)
    sums = swap(triangle(swap(sent), 0))
    return call(last_kernel, struct(pair.shape, F32), [held], [VMEM] * 4, 2 * 2048 * 128 * 128)(
        sums, turned, gating, in_final
    )


def solution(mesh):
    placed = (P("row", "col", None), P(), P(), P(), P(), P())
    return jax.shard_map(
        shards, mesh=mesh, in_specs=placed, out_specs=P("row", "col", None), check_vma=False
    )
```

time: 449 us -> 105 us (0.23)
  waiting for transfers between devices: 315 us -> 23.9 us
  local copies, waits for them, and re-layouts: 64.5 us -> 6.32 us
  blocking collectives: 0 us -> 53.6 us
  matrix products: 36.3 us -> 0 us
  other arithmetic: 16.9 us -> 0 us
  between operations: 13.3 us -> 0.13 us
  Pallas kernels: 0 us -> 11.5 us
  starting transfers between devices: 0.53 us -> 9.21 us
    reduce_scatter x2 -> x0, waiting for transfers between devices: 190 us -> none  [the longest x1 100 us: shards(): lax.psum_scatter(partial_sums.astype(jnp.bfloat16), 'row', scatter_dimens...]
    all_gather x2 -> x0, waiting for transfers between devices: 124 us -> none  [the longest x1 74.8 us: shards(): lax.all_gather(right_side, 'row', axis=0, tiled=True)]
    all_to_all x0 -> x2, blocking collectives: none -> 53.6 us  [swap(): return lax.all_to_all(values, axes, 0, 0, tiled=True)]
    dot_general x6 -> x0, matrix products: 36.3 us -> none  [the longest x1 11.3 us: shards(): jnp.einsum('ikc,jkc->ijc', left_side, lax.all_gather(right_side, 'row', a...]
    all_gather x2 -> x0, local copies, waits for them, and re-layouts: 31.6 us -> none  [the longest x1 23.7 us: shards(): lax.all_gather(right_side, 'row', axis=0, tiled=True)]
    all_to_all x0 -> x2, waiting for transfers between devices: none -> 23.9 us  [swap(): return lax.all_to_all(values, axes, 0, 0, tiled=True)]
    convert_element_type x3 -> x0, local copies, waits for them, and re-layouts: 16.9 us -> none  [the longest x1 13.7 us: shards(): partial_sums.astype(jnp.bfloat16)]
    pallas_call x0 -> x7, Pallas kernels: none -> 11.5 us  [the longest x2 3.5 us: triangle(): call(kernel, answer, [operand, operand], [VMEM], 2 * 512 ** 3)]
  transfers between devices with their start and end apart: 4 -> 2, of which waited for: 4 -> 2; matrix products, arithmetic and copies ran while one was open for 1% -> 0% of each run, Pallas kernels for 0% -> 1%
where the time goes in v1:
time: 105 us
  blocking collectives  53.6 us (51%)
  waiting for transfers between devices  23.9 us (23%)
  Pallas kernels  11.5 us (11%)
  starting transfers between devices  9.21 us (9%)
  local copies, waits for them, and re-layouts  6.32 us (6%)
    all_to_all x2, blocking collectives, swap(): return lax.all_to_all(values, axes, 0, 0, tiled=True)  53.6 us
    all_to_all x2, waiting for transfers between devices, swap(): return lax.all_to_all(values, axes, 0, 0, tiled=True)  23.9 us
    all_to_all x2, starting transfers between devices, swap(): return lax.all_to_all(values, axes, 0, 0, tiled=True)  9.21 us
    unnamed x26, local copies, waits for them, and re-layouts  6.32 us
    pallas_call x2, Pallas kernels, triangle(): call(kernel, answer, [operand, operand], [VMEM], 2 * 512 ** 3)  3.5 us
    pallas_call x1, Pallas kernels, shards(): call(middle_kernel, (message, whole), [held, held], [SMEM] + [VMEM] * 6,...  2.94 us
  transfers between devices with their start and end apart: 2, of which 2 were waited for; matrix products, arithmetic and copies ran while one was open for 0% of the time, Pallas kernels for 1%

profile of v1, /device:TPU:1, one launch (start us, length us, event | category | flops | bytes accessed | tf_op | source)
XLA Modules:
  0.0 104.7 jit_solution(10675199755874572817)
XLA Ops:
  0.0 0.0 copy-start
  0.0 1.2 %copy-done = f32[32,64,128]{2,1,0:T(8,128)S(1)} copy-done((f32[32,64,128]{2,1,0:T(8,128)S(1)}, f32[32,64,128]{2,1,0:T(8,128)}, u32[]{:S(2)}) %copy-start) | copy-done | bytes 1048600
  1.2 0.0 copy-start.2
  1.2 1.0 copy-done.2
  2.2 0.0 copy-start.11
  2.2 0.7 copy-done.11
  2.9 2.0 %shard_map.64 = bf16[128,32,128]{2,1,0:T(8,128)(2,1)S(1)} custom-call(s32[512]{0:T(512)S(1)} %copy-done.11, s32[4,128]{1,0:T(4,128)S(1)} %bitcast.7, f32[32,64,128]{2,1,0:T(8,128)S(1)} %copy-done, f32[128,640]{1,0:T(8,128)S(1)} %copy-done.2), custom_call_target="tpu_custom_call" | custom-call | flops 268435456 | bytes 3145728 | tf_op jit(solution)/shard_map/pallas_call | solution.py:205
  4.9 30.4 %all_to_all.20 = bf16[128,32,128]{2,1,0:T(8,128)(2,1)S(1)} all-to-all(bf16[128,32,128]{2,1,0:T(8,128)(2,1)S(1)} %shard_map.64), channel_id=1, replica_groups=mesh['row'=16,'col'=8] {'row','col'}, dimensions={0} | all-to-all | bytes 2097152 | tf_op jit(solution)/shard_map/all_to_all | solution.py:198
  35.3 0.0 copy-start.1
  35.3 1.8 %shard_map.65 = bf16[16,8,16,128]{3,2,1,0:T(8,128)(2,1)} custom-call(bf16[16,8,32,128]{3,2,1,0:T(8,128)(2,1)S(1)} %bitcast.5), custom_call_target="tpu_custom_call" | custom-call | flops 268435456 | bytes 3145728 | tf_op jit(solution)/shard_map/pallas_call | solution.py:202
  37.2 0.0 copy-start.3
  37.2 4.7 %all-to-all-start.1 = ((bf16[128,16,128]{2,1,0:T(8,128)(2,1)}), bf16[128,16,128]{2,1,0:T(8,128)(2,1)S(1)}, u32[]{:S(2)}, u32[]{:S(2)}) async-start(bf16[128,16,128]{2,1,0:T(8,128)(2,1)} %bitcast.2), calls=%async_computation.1 | async-start | bytes 1048576 | tf_op jit(solution)/shard_map/all_to_all | solution.py:198
  41.9 0.0 copy-done.1
  41.9 0.0 copy-done.3
  41.9 0.0 copy-start.4
  41.9 0.0 copy-start.10
  41.9 0.6 shard_map.66
  42.6 0.0 copy-start.7
  42.6 1.0 copy-done.7
  43.5 0.0 copy-start.12
  43.5 12.0 %all-to-all-done.1.got = bf16[128,16,128]{2,1,0:T(8,128)(2,1)S(1)} async-done(((bf16[128,16,128]{2,1,0:T(8,128)(2,1)}), bf16[128,16,128]{2,1,0:T(8,128)(2,1)S(1)}, u32[]{:S(2)}, u32[]{:S(2)}) %all-to-all-start.1) | async-done | bytes 524320 | tf_op jit(solution)/shard_map/all_to_all | solution.py:198
  55.6 0.0 copy-done.4
  55.6 0.0 copy-done.10
  55.6 0.0 copy-done.12
  55.6 0.0 copy-start.8
  55.6 1.2 %copy-done.8 = f32[128,2048]{1,0:T(8,128)S(1)} copy-done((f32[128,2048]{1,0:T(8,128)S(1)}, f32[128,2048]{1,0:T(8,128)}, u32[]{:S(2)}) %copy-start.8) | copy-done | bytes 1048600
  56.8 2.9 %shard_map.67 = (bf16[128,32,128]{2,1,0:T(8,128)(2,1)S(1)}, f32[128,2048]{1,0:T(8,128)S(1)}) custom-call(s32[512]{0:T(512)S(1)} %copy-done.12, s32[4,128]{1,0:T(4,128)S(1)} %bitcast.8, bf16[128,16,128]{2,1,0:T(8,128)(2,1)S(1)} %all-to-all-done.1.got, f32[128,2048]{1,0:T(8,128)S(1)} %get-tuple-element.11.flat, f32[128,2048]{1,0:T(8,128)S(1)} %copy-done.8, ...), custom_call_target="tpu_custom_call" | custom-call | flops 335544320 | bytes 3145728 | tf_op jit(solution)/shard_map/pallas_call | solution.py:210
  59.8 0.0 copy-start.5
  59.8 23.2 %all_to_all.21 = bf16[128,32,128]{2,1,0:T(8,128)(2,1)S(1)} all-to-all(bf16[128,32,128]{2,1,0:T(8,128)(2,1)S(1)} %get-tuple-element.13), channel_id=1, replica_groups=mesh['row'=16,'col'=8] {'row','col'}, dimensions={0} | all-to-all | bytes 2097152 | tf_op jit(solution)/shard_map/all_to_all | solution.py:198
  83.0 0.0 copy-done.5
  83.0 1.7 %shard_map.68 = bf16[16,8,16,128]{3,2,1,0:T(8,128)(2,1)} custom-call(bf16[16,8,32,128]{3,2,1,0:T(8,128)(2,1)S(1)} %bitcast.6), custom_call_target="tpu_custom_call" | custom-call | flops 268435456 | bytes 3145728 | tf_op jit(solution)/shard_map/pallas_call | solution.py:202
  84.6 4.5 %all-to-all-start.3 = ((bf16[128,16,128]{2,1,0:T(8,128)(2,1)}), bf16[128,16,128]{2,1,0:T(8,128)(2,1)S(1)}, u32[]{:S(2)}, u32[]{:S(2)}) async-start(bf16[128,16,128]{2,1,0:T(8,128)(2,1)} %bitcast.4), calls=%async_computation.3 | async-start | bytes 1048576 | tf_op jit(solution)/shard_map/all_to_all | solution.py:198
  89.2 0.0 copy-start.6
  89.2 1.2 %copy-done.6 = f32[128,2048]{1,0:T(8,128)S(1)} copy-done((f32[128,2048]{1,0:T(8,128)S(1)}, f32[128,2048]{1,0:T(8,128)}, u32[]{:S(2)}) %copy-start.6) | copy-done | bytes 1048600
  90.4 0.0 copy-start.9
  90.4 0.6 shard_map.69
  91.0 11.9 %all-to-all-done.3.got = bf16[128,16,128]{2,1,0:T(8,128)(2,1)S(1)} async-done(((bf16[128,16,128]{2,1,0:T(8,128)(2,1)}), bf16[128,16,128]{2,1,0:T(8,128)(2,1)S(1)}, u32[]{:S(2)}, u32[]{:S(2)}) %all-to-all-start.3) | async-done | bytes 524320 | tf_op jit(solution)/shard_map/all_to_all | solution.py:198
  102.9 0.0 copy-done.9
  102.9 1.8 %shard_map.70 = f32[32,64,128]{2,1,0:T(8,128)} custom-call(bf16[128,16,128]{2,1,0:T(8,128)(2,1)S(1)} %all-to-all-done.3.got, f32[16,128,128]{2,1,0:T(8,128)S(1)} %get-tuple-element.15.turned, f32[16,128,128]{2,1,0:T(8,128)S(1)} %get-tuple-element.16.gating, f32[128,128]{1,0:T(8,128)S(1)} %copy-done.9), custom_call_target="tpu_custom_call" | custom-call | flops 67108864 | bytes 3145728 | tf_op jit(solution)/shard_map/pallas_call | solution.py:216
Async XLA Ops:
  0.0 1.2 %copy-start = (f32[32,64,128]{2,1,0:T(8,128)S(1)}, f32[32,64,128]{2,1,0:T(8,128)}, u32[]{:S(2)}) copy-start(f32[32,64,128]{2,1,0:T(8,128)} %pair.3) | copy-start | bytes 3145732
  1.2 1.0 copy-start.2
  2.2 0.7 copy-start.11
  35.3 6.5 %copy-start.1 = (f32[32,64,128]{2,1,0:T(8,128)S(1)}, f32[32,64,128]{2,1,0:T(8,128)}, u32[]{:S(2)}) copy-start(f32[32,64,128]{2,1,0:T(8,128)} %pair.3) | copy-start | bytes 3145732
  37.2 4.7 %copy-start.3 = (f32[128,640]{1,0:T(8,128)S(1)}, f32[128,640]{1,0:T(8,128)}, u32[]{:S(2)}) copy-start(f32[128,640]{1,0:T(8,128)} %proj.5) | copy-start | bytes 983044
  37.2 18.4 %all-to-all-start.1 = ((bf16[128,16,128]{2,1,0:T(8,128)(2,1)}), bf16[128,16,128]{2,1,0:T(8,128)(2,1)S(1)}, u32[]{:S(2)}, u32[]{:S(2)}) async-start(bf16[128,16,128]{2,1,0:T(8,128)(2,1)} %bitcast.2), calls=%async_computation.1 | async-start | bytes 1048576 | tf_op jit(solution)/shard_map/all_to_all | solution.py:198
  41.9 13.7 %copy-start.4 = (f32[128,640]{1,0:T(8,128)S(1)}, f32[128,640]{1,0:T(8,128)}, u32[]{:S(2)}) copy-start(f32[128,640]{1,0:T(8,128)} %proj.7) | copy-start | bytes 983044
  41.9 13.7 %copy-start.10 = (f32[128,128]{1,0:T(8,128)S(1)}, f32[128,128]{1,0:T(8,128)}, u32[]{:S(2)}) copy-start(f32[128,128]{1,0:T(8,128)} %final.2) | copy-start | bytes 196612
  42.6 1.0 copy-start.7
  43.5 12.1 %copy-start.12 = (s32[512]{0:T(512)S(1)}, s32[512]{0:T(512)}, u32[]{:S(2)}) copy-start(s32[512]{0:T(512)} %token_s.3) | copy-start | bytes 6148
  55.6 1.2 %copy-start.8 = (f32[128,2048]{1,0:T(8,128)S(1)}, f32[128,2048]{1,0:T(8,128)}, u32[]{:S(2)}) copy-start(f32[128,2048]{1,0:T(8,128)} %copy-done.7) | copy-start | bytes 3145732
  59.8 23.2 %copy-start.5 = (f32[128,2048]{1,0:T(8,128)}, f32[128,2048]{1,0:T(8,128)S(1)}, u32[]{:S(2)}) copy-start(f32[128,2048]{1,0:T(8,128)S(1)} %get-tuple-element.14.first) | copy-start | bytes 3145732
  84.6 18.3 %all-to-all-start.3 = ((bf16[128,16,128]{2,1,0:T(8,128)(2,1)}), bf16[128,16,128]{2,1,0:T(8,128)(2,1)S(1)}, u32[]{:S(2)}, u32[]{:S(2)}) async-start(bf16[128,16,128]{2,1,0:T(8,128)(2,1)} %bitcast.4), calls=%async_computation.3 | async-start | bytes 1048576 | tf_op jit(solution)/shard_map/all_to_all | solution.py:198
  89.2 1.2 %copy-start.6 = (f32[128,2048]{1,0:T(8,128)S(1)}, f32[128,2048]{1,0:T(8,128)}, u32[]{:S(2)}) copy-start(f32[128,2048]{1,0:T(8,128)} %copy-done.5) | copy-start | bytes 3145732
  90.4 12.5 %copy-start.9 = (f32[128,128]{1,0:T(8,128)S(1)}, f32[128,128]{1,0:T(8,128)}, u32[]{:S(2)}) copy-start(f32[128,128]{1,0:T(8,128)} %final.3) | copy-start | bytes 196612

commit v2 on v1

v2 whole, which is shorter than its diff:
```python
import functools

import jax
import jax.numpy as jnp
from jax import lax
from jax.experimental import pallas as pl
from jax.experimental.pallas import tpu as pltpu
from jax.sharding import PartitionSpec as P

HALF = 64
TILES = 16
F32 = jnp.float32
BF16 = jnp.bfloat16
VMEM = pl.BlockSpec(memory_space=pltpu.VMEM)
SMEM = pl.BlockSpec(memory_space=pltpu.SMEM)
HBM = pl.BlockSpec(memory_space=pltpu.HBM)


def call(kernel, outs, scratch, specs, flops, limit=16):
    return pl.pallas_call(
        kernel,
        out_shape=outs,
        in_specs=specs,
        out_specs=jax.tree.map(lambda _: VMEM, outs),
        scratch_shapes=scratch,
        compiler_params=pltpu.CompilerParams(vmem_limit_bytes=limit * 1024 * 1024),
        cost_estimate=pl.CostEstimate(flops=flops, bytes_accessed=3 << 20, transcendentals=1 << 19),
    )


def low_lanes(shape):
    return lax.broadcasted_iota(jnp.int32, shape, len(shape) - 1) < HALF


def turn(values):
    return pltpu.roll(values, HALF, axis=values.ndim - 1)


def norm(values, mask=None):
    scale = 1.0 / values.shape[0]
    centred = values - jnp.sum(values, axis=0, keepdims=True) * scale
    factor = lax.rsqrt(jnp.sum(centred * centred, axis=0, keepdims=True) * scale + 1e-05)
    return centred * (factor if mask is None else factor * mask)


def dot(left, right, dims=((1,), (0,))):
    return lax.dot_general(left, right, (dims, ((), ())), preferred_element_type=F32)


def halved(weights):
    parts = [weights[:, k : k + 128].T for k in range(0, weights.shape[1], 128)]
    return (jnp.concatenate(parts, axis=0) * 0.5).astype(BF16)


def masks(token_s, token_v):
    row = lax.axis_index("row")
    col = lax.axis_index("col")
    line = token_v[pl.ds(col // 2, 1), :].astype(F32)
    low = low_lanes((1, 128))
    odd = col % 2
    pick = jnp.where(low, 1, 0) != odd
    cols = jnp.where(pick, line, turn(line))

    def of_tile(tile):
        first = row * 32 + (tile // 8) * 16 + tile % 8
        top = token_s(first).astype(F32)
        bottom = token_s(first + 8).astype(F32)
        return cols * jnp.where(low, top, bottom)

    return lambda tile: jnp.concatenate([of_tile(tile), of_tile(tile + 1)], axis=1)


def pair_tile(pair, tile):
    first = (tile // 8) * 16 + tile % 8
    return jnp.concatenate([pair[first], pair[first + 8]], axis=0).T


def sides(normed, weights, held, slot):
    linear = dot(weights, normed.astype(BF16))
    left = ((1.0 + jnp.tanh(linear[128:256])) * linear[0:128]).astype(BF16)
    right = ((1.0 + jnp.tanh(linear[384:512])) * linear[256:384]).astype(BF16)
    for k in range(2):
        low = slice(128 * k, 128 * k + HALF)
        high = slice(128 * k + HALF, 128 * (k + 1))
        held[slot + k] = jnp.concatenate([left[:, low], right[:, low]], axis=1)
        held[slot + k + 8] = jnp.concatenate([left[:, high], right[:, high]], axis=1)
    return 1.0 + jnp.tanh(linear[512:640])


def pack(held, out, group):
    for k in range(0, 128, 32):
        out[k : k + 32, 16 * group : 16 * group + 16, :] = jnp.swapaxes(held[:, k : k + 32, :], 0, 1)


def project_kernel(
    token_h, pair_h, proj_h, out, flat, gating, held, token_s, token_v, pair, proj, semaphores
):
    rows = [(8 * k + 4 * part, 4) for k in (0, 2) for part in (0, 1)]
    rows = [(first + step, 4) for first, _ in rows for step in (0, 8)]
    copies = [
        pltpu.make_async_copy(pair_h.at[pl.ds(first, n)], pair.at[pl.ds(first, n)], semaphores.at[k])
        for k, (first, n) in enumerate(rows)
    ]
    others = [
        pltpu.make_async_copy(proj_h, proj, semaphores.at[8]),
        pltpu.make_async_copy(token_h, token_s, semaphores.at[9]),
        pltpu.make_async_copy(token_h, token_v, semaphores.at[10]),
    ]
    for copy in others + copies:
        copy.start()
    others[0].wait()
    weights = halved(proj)
    others[1].wait()
    others[2].wait()
    mask = masks(lambda n: token_s[n // 128, n % 128], token_v)
    for group in range(2):
        for slot in range(0, 8, 2):
            if slot % 4 == 0:
                for copy in copies[4 * group + slot // 2 : 4 * group + slot // 2 + 2]:
                    copy.wait()
            tile = 8 * group + slot
            lanes = slice(128 * tile, 128 * (tile + 2))
            values = jnp.concatenate([pair_tile(pair, tile), pair_tile(pair, tile + 1)], axis=1)
            flat[:, lanes] = values
            gating[:, lanes] = sides(norm(values, mask(tile)), weights, held, slot)
        pack(held, out, group)


def operands(got, left, right):
    for k in range(4):
        lanes = slice(128 * k, 128 * (k + 1))
        even = got[:, 2 * k].reshape(512, 128)
        odd = got[:, 2 * k + 1].reshape(512, 128)
        left[:, lanes] = jnp.concatenate([even[:, :HALF], odd[:, :HALF]], axis=1)
        right[:, lanes] = jnp.concatenate([even[:, HALF:], odd[:, HALF:]], axis=1)


def triangle_kernel(contract, got, out, left, right):
    operands(got, left, right)
    low = low_lanes((16, 128))
    for k in range(0, 16, 4):
        rows = slice(32 * k, 32 * (k + 4))
        if contract == 1:
            sums = dot(left[rows, :], right[...], ((1,), (1,)))
        else:
            sums = dot(left[:, rows], right[...], ((0,), (0,)))
        sums = sums.reshape(4, 2, 2, 8, 512)
        for n in range(4):
            for m in range(4):
                lanes = slice(128 * m, 128 * (m + 1))
                top = sums[n, :, 0, :, lanes].reshape(16, 128)
                bottom = sums[n, :, 1, :, lanes].reshape(16, 128)
                out[k + n, 2 * m] = jnp.where(low, top, turn(bottom)).astype(BF16)
                out[k + n, 2 * m + 1] = jnp.where(low, turn(top), bottom).astype(BF16)


def unpack(got, triangle):
    for k in range(0, 128, 32):
        triangle[:, k : k + 32, :] = jnp.swapaxes(got[k : k + 32], 0, 1)


def finish(triangle, tile, flat, gating, closing):
    lanes = slice(128 * tile, 128 * (tile + 2))
    sums = jnp.concatenate([triangle[tile], triangle[tile + 1]], axis=1).astype(F32)
    return flat[:, lanes] + gating[:, lanes] * dot(closing, norm(sums).astype(BF16))


def middle_kernel(
    token_s, token_v, got, flat, gating, final, proj, out, first, next_gating, held, triangle
):
    weights = halved(proj)
    closing = halved(final)
    mask = masks(lambda n: token_s[n // 128, n % 128], token_v)
    unpack(got, triangle)
    for group in range(2):
        for slot in range(0, 8, 2):
            tile = 8 * group + slot
            lanes = slice(128 * tile, 128 * (tile + 2))
            values = finish(triangle, tile, flat, gating, closing)
            first[:, lanes] = values
            next_gating[:, lanes] = sides(norm(values, mask(tile)), weights, held, slot)
        pack(held, out, group)


def last_kernel(got, first, gating, final, out, triangle, done, semaphores):
    closing = halved(final)
    unpack(got, triangle)
    copies = []
    for tile in range(0, TILES, 2):
        values = finish(triangle, tile, first, gating, closing)
        row = (tile // 8) * 16 + tile % 8
        for k in range(2):
            part = values[:, 128 * k : 128 * (k + 1)].T
            done[row + k] = part[:HALF]
            done[row + k + 8] = part[HALF:]
        if tile % 4 == 2:
            for start in (row - 2, row + 6):
                copies.append(
                    pltpu.make_async_copy(
                        done.at[pl.ds(start, 4)], out.at[pl.ds(start, 4)], semaphores.at[len(copies)]
                    )
                )
                copies[-1].start()
    for copy in copies:
        copy.wait()


def shards(pair, token_mask, out_proj, out_final, in_proj, in_final):
    axes = ("row", "col")
    struct = jax.ShapeDtypeStruct
    lines = token_mask.reshape(4, 128)
    message = struct((128, 32, 128), BF16)
    answer = struct((16, 8, 16, 128), BF16)
    whole = struct((128, 2048), F32)
    held = pltpu.VMEM((16, 128, 128), BF16)
    operand = pltpu.VMEM((512, 512), BF16)

    def swap(values):
        return lax.all_to_all(values, axes, 0, 0, tiled=True)

    def triangle(got, contract):
        kernel = functools.partial(triangle_kernel, contract)
        sums = call(kernel, answer, [operand, operand], [VMEM], 2 * 512**3)(got.reshape(16, 8, 32, 128))
        return sums.reshape(128, 16, 128)

    scratch = [
        held,
        pltpu.SMEM((4, 128), jnp.int32),
        pltpu.VMEM((4, 128), jnp.int32),
        pltpu.VMEM(pair.shape, F32),
        pltpu.VMEM(out_proj.shape, F32),
        pltpu.SemaphoreType.DMA((11,)),
    ]
    sent, flat, gating = call(
        project_kernel, (message, whole, whole), scratch, [HBM] * 3, 2 * 2048 * 128 * 640
    )(*[pltpu.with_memory_space_constraint(v, pltpu.HBM) for v in (lines, pair, out_proj)])
    sums = swap(triangle(swap(sent), 1))
    sent, first, gating = call(
        middle_kernel, (message, whole, whole), [held, held], [SMEM] + [VMEM] * 6, 2 * 2048 * 128 * 768
    )(lines, lines, sums, flat, gating, out_final, in_proj)
    sums = swap(triangle(swap(sent), 0))
    return pl.pallas_call(
        last_kernel,
        out_shape=struct(pair.shape, F32),
        in_specs=[VMEM] * 4,
        out_specs=HBM,
        scratch_shapes=[held, pltpu.VMEM(pair.shape, F32), pltpu.SemaphoreType.DMA((8,))],
        compiler_params=pltpu.CompilerParams(vmem_limit_bytes=16 * 1024 * 1024),
        cost_estimate=pl.CostEstimate(flops=2 * 2048 * 128 * 128, bytes_accessed=3 << 20, transcendentals=0),
    )(sums, first, gating, in_final)


def solution(mesh):
    placed = (P("row", "col", None), P(), P(), P(), P(), P())
    return jax.shard_map(
        shards, mesh=mesh, in_specs=placed, out_specs=P("row", "col", None), check_vma=False
    )
```

time: 105 us -> 100 us (0.952)
  blocking collectives: 53.6 us -> 89.2 us
  waiting for transfers between devices: 23.9 us -> 0 us
  starting transfers between devices: 9.21 us -> 0 us
  local copies, waits for them, and re-layouts: 6.32 us -> 0.7 us
  Pallas kernels: 11.5 us -> 10.2 us
    all_to_all x2 -> x4, blocking collectives: 53.6 us -> 89.2 us  [swap(): return lax.all_to_all(values, axes, 0, 0, tiled=True)]
    all_to_all x2 -> x0, waiting for transfers between devices: 23.9 us -> none  [swap(): return lax.all_to_all(values, axes, 0, 0, tiled=True)]
    all_to_all x2 -> x0, starting transfers between devices: 9.21 us -> none  [swap(): return lax.all_to_all(values, axes, 0, 0, tiled=True)]
    unnamed x26 -> x8, local copies, waits for them, and re-layouts: 6.32 us -> 0.7 us
    pallas_call x2, Pallas kernels: 3.5 us -> 1.89 us  [triangle(): call(kernel, answer, [operand, operand], [VMEM], 2 * 512 ** 3)]
    pallas_call x5 -> x3, Pallas kernels: 7.98 us -> 8.29 us  [the longest x1 3.87 us: shards(): call(project_kernel, (message, whole, whole), scratch, [HBM] * 3, 2 * 204...]
  transfers between devices with their start and end apart: 2 -> 0, of which waited for: 2 -> 0; matrix products, arithmetic and copies ran while one was open for 0% -> 0% of each run, Pallas kernels for 1% -> 0%
where the time goes in v2:
time: 100 us
  blocking collectives  89.2 us (89%)
  Pallas kernels  10.2 us (10%)
    all_to_all x4, blocking collectives, swap(): return lax.all_to_all(values, axes, 0, 0, tiled=True)  89.2 us
    pallas_call x1, Pallas kernels, shards(): call(project_kernel, (message, whole, whole), scratch, [HBM] * 3, 2 * 204...  3.87 us
    pallas_call x1, Pallas kernels, shards(): call(middle_kernel, (message, whole, whole), [held, held], [SMEM] + [VMEM...  2.78 us

profile of v2, /device:TPU:1, one launch (start us, length us, event | category | flops | bytes accessed | tf_op | source)
XLA Modules:
  0.0 100.1 jit_solution(6245433640658527617)
XLA Ops:
  0.0 3.9 %shard_map.64 = (bf16[128,32,128]{2,1,0:T(8,128)(2,1)S(1)}, f32[128,2048]{1,0:T(8,128)S(1)}, f32[128,2048]{1,0:T(8,128)S(1)}) custom-call(s32[4,128]{1,0:T(4,128)} %bitcast.9, f32[32,64,128]{2,1,0:T(8,128)} %pair_h.1, f32[128,640]{1,0:T(8,128)} %proj_h.1), custom_call_target="tpu_custom_call" | custom-call | flops 335544320 | bytes 3145728 | tf_op jit(solution)/shard_map/pallas_call | solution.py:234
  3.9 30.4 %all_to_all.20 = bf16[128,32,128]{2,1,0:T(8,128)(2,1)S(1)} all-to-all(bf16[128,32,128]{2,1,0:T(8,128)(2,1)S(1)} %get-tuple-element.11), channel_id=1, replica_groups=mesh['row'=16,'col'=8] {'row','col'}, dimensions={0} | all-to-all | bytes 2097152 | tf_op jit(solution)/shard_map/all_to_all | solution.py:219
  34.3 1.0 %shard_map.65 = bf16[16,8,16,128]{3,2,1,0:T(8,128)(2,1)S(1)} custom-call(bf16[16,8,32,128]{3,2,1,0:T(8,128)(2,1)S(1)} %bitcast.5), custom_call_target="tpu_custom_call" | custom-call | flops 268435456 | bytes 3145728 | tf_op jit(solution)/shard_map/pallas_call | solution.py:223
  35.3 0.0 copy-start
  35.4 0.0 copy-start.2
  35.4 17.8 %all_to_all.21.got = bf16[128,16,128]{2,1,0:T(8,128)(2,1)S(1)} all-to-all(bf16[128,16,128]{2,1,0:T(8,128)(2,1)S(1)} %bitcast.7), channel_id=1, replica_groups=mesh['row'=16,'col'=8] {'row','col'}, dimensions={0} | all-to-all | bytes 1048576 | tf_op jit(solution)/shard_map/all_to_all | solution.py:219
  53.1 0.0 copy-start.3
  53.1 0.0 copy-done
  53.1 0.0 copy-done.2
  53.1 0.7 copy-done.3
  53.8 2.8 %shard_map.66 = (bf16[128,32,128]{2,1,0:T(8,128)(2,1)S(1)}, f32[128,2048]{1,0:T(8,128)S(1)}, f32[128,2048]{1,0:T(8,128)S(1)}) custom-call(s32[4,128]{1,0:T(4,128)S(1)} %bitcast.10, s32[4,128]{1,0:T(4,128)S(1)} %bitcast.11, bf16[128,16,128]{2,1,0:T(8,128)(2,1)S(1)} %all_to_all.21.got, f32[128,2048]{1,0:T(8,128)S(1)} %get-tuple-element.12.flat, ...), custom_call_target="tpu_custom_call" | custom-call | flops 402653184 | bytes 3145728 | tf_op jit(solution)/shard_map/pallas_call | solution.py:238
  56.6 23.2 %all_to_all.22 = bf16[128,32,128]{2,1,0:T(8,128)(2,1)S(1)} all-to-all(bf16[128,32,128]{2,1,0:T(8,128)(2,1)S(1)} %get-tuple-element.14), channel_id=1, replica_groups=mesh['row'=16,'col'=8] {'row','col'}, dimensions={0} | all-to-all | bytes 2097152 | tf_op jit(solution)/shard_map/all_to_all | solution.py:219
  79.8 0.9 shard_map.67
  80.7 0.0 copy-start.1
  80.7 17.8 %all_to_all.23.got = bf16[128,16,128]{2,1,0:T(8,128)(2,1)S(1)} all-to-all(bf16[128,16,128]{2,1,0:T(8,128)(2,1)S(1)} %bitcast.8), channel_id=1, replica_groups=mesh['row'=16,'col'=8] {'row','col'}, dimensions={0} | all-to-all | bytes 1048576 | tf_op jit(solution)/shard_map/all_to_all | solution.py:219
  98.4 0.0 copy-done.1
  98.4 1.6 %shard_map.68 = f32[32,64,128]{2,1,0:T(8,128)} custom-call(bf16[128,16,128]{2,1,0:T(8,128)(2,1)S(1)} %all_to_all.23.got, f32[128,2048]{1,0:T(8,128)S(1)} %get-tuple-element.15.first, f32[128,2048]{1,0:T(8,128)S(1)} %get-tuple-element.16.gating, f32[128,128]{1,0:T(8,128)S(1)} %copy-done.1), custom_call_target="tpu_custom_call" | custom-call | flops 67108864 | bytes 3145728 | tf_op jit(solution)/shard_map/pallas_call | solution.py:242
Async XLA Ops:
  35.3 17.8 %copy-start = (f32[128,640]{1,0:T(8,128)S(1)}, f32[128,640]{1,0:T(8,128)}, u32[]{:S(2)}) copy-start(f32[128,640]{1,0:T(8,128)} %proj.1) | copy-start | bytes 983044
  35.4 17.8 %copy-start.2 = (f32[128,128]{1,0:T(8,128)S(1)}, f32[128,128]{1,0:T(8,128)}, u32[]{:S(2)}) copy-start(f32[128,128]{1,0:T(8,128)} %final.2) | copy-start | bytes 196612
  53.1 0.7 copy-start.3
  80.7 17.8 %copy-start.1 = (f32[128,128]{1,0:T(8,128)S(1)}, f32[128,128]{1,0:T(8,128)}, u32[]{:S(2)}) copy-start(f32[128,128]{1,0:T(8,128)} %final.3) | copy-start | bytes 196612

commit v3 on v2

--- a/solution.py
+++ b/solution.py
@@ -52,27 +52,27 @@
     return (jnp.concatenate(parts, axis=0) * 0.5).astype(BF16)
 
 
-def masks(token_s, token_v):
+def masks(tokens):
     row = lax.axis_index("row")
     col = lax.axis_index("col")
-    line = token_v[pl.ds(col // 2, 1), :].astype(F32)
-    low = low_lanes((1, 128))
-    odd = col % 2
-    pick = jnp.where(low, 1, 0) != odd
+    line = tokens[pl.ds(col // 2, 1), :].astype(F32)
+    pick = jnp.where(low_lanes((1, 128)), 1, 0) != col % 2
     cols = jnp.where(pick, line, turn(line))
-
-    def of_tile(tile):
-        first = row * 32 + (tile // 8) * 16 + tile % 8
-        top = token_s(first).astype(F32)
-        bottom = token_s(first + 8).astype(F32)
-        return cols * jnp.where(low, top, bottom)
-
-    return lambda tile: jnp.concatenate([of_tile(tile), of_tile(tile + 1)], axis=1)
+    line = jnp.broadcast_to(tokens[pl.ds(row // 4, 1), :].astype(F32), (32, 128))
+    lane = lax.broadcasted_iota(jnp.int32, (32, 128), 1)
+    own = lax.broadcasted_iota(jnp.int32, (32, 128), 0) + 32 * (row % 4)
+    rows = jnp.sum(jnp.where(lane == own, line, 0.0), axis=1, keepdims=True) * cols
+    low = low_lanes((8, 128))
+    return jnp.concatenate([jnp.where(low, rows[k : k + 8], rows[k + 8 : k + 16]) for k in (0, 16)], axis=0)
+
+
+def mask_of(mask, tile):
+    return jnp.concatenate([mask[tile : tile + 1], mask[tile + 1 : tile + 2]], axis=1)
 
 
 def pair_tile(pair, tile):
-    first = (tile // 8) * 16 + tile % 8
-    return jnp.concatenate([pair[first], pair[first + 8]], axis=0).T
+    place = (tile // 8, slice(None), tile % 8 // 4, tile % 4)
+    return pair[place].reshape(128, 128).T
 
 
 def sides(normed, weights, held, slot):
@@ -92,37 +92,29 @@
         out[k : k + 32, 16 * group : 16 * group + 16, :] = jnp.swapaxes(held[:, k : k + 32, :], 0, 1)
 
 
-def project_kernel(
-    token_h, pair_h, proj_h, out, flat, gating, held, token_s, token_v, pair, proj, semaphores
-):
-    rows = [(8 * k + 4 * part, 4) for k in (0, 2) for part in (0, 1)]
-    rows = [(first + step, 4) for first, _ in rows for step in (0, 8)]
+def project_kernel(token_h, pair_h, proj_h, out, flat, gating, mask, held, tokens, pair, proj, semaphores):
+    parts = [(group, slice(None), part) for group in (0, 1) for part in (0, 1)]
     copies = [
-        pltpu.make_async_copy(pair_h.at[pl.ds(first, n)], pair.at[pl.ds(first, n)], semaphores.at[k])
-        for k, (first, n) in enumerate(rows)
+        pltpu.make_async_copy(pair_h.at[part], pair.at[part], semaphores.at[k])
+        for k, part in enumerate(parts)
     ]
-    others = [
-        pltpu.make_async_copy(proj_h, proj, semaphores.at[8]),
-        pltpu.make_async_copy(token_h, token_s, semaphores.at[9]),
-        pltpu.make_async_copy(token_h, token_v, semaphores.at[10]),
-    ]
-    for copy in others + copies:
+    weight_copy = pltpu.make_async_copy(proj_h, proj, semaphores.at[4])
+    token_copy = pltpu.make_async_copy(token_h, tokens, semaphores.at[5])
+    for copy in [weight_copy, token_copy] + copies:
         copy.start()
-    others[0].wait()
+    for copy in copies:
+        copy.wait()
+    weight_copy.wait()
+    token_copy.wait()
     weights = halved(proj)
-    others[1].wait()
-    others[2].wait()
-    mask = masks(lambda n: token_s[n // 128, n % 128], token_v)
+    mask[...] = masks(tokens)
     for group in range(2):
         for slot in range(0, 8, 2):
-            if slot % 4 == 0:
-                for copy in copies[4 * group + slot // 2 : 4 * group + slot // 2 + 2]:
-                    copy.wait()
             tile = 8 * group + slot
             lanes = slice(128 * tile, 128 * (tile + 2))
             values = jnp.concatenate([pair_tile(pair, tile), pair_tile(pair, tile + 1)], axis=1)
             flat[:, lanes] = values
-            gating[:, lanes] = sides(norm(values, mask(tile)), weights, held, slot)
+            gating[:, lanes] = sides(norm(values, mask_of(mask, tile)), weights, held, slot)
         pack(held, out, group)
 
 
@@ -166,11 +158,10 @@
 
 
 def middle_kernel(
-    token_s, token_v, got, flat, gating, final, proj, out, first, next_gating, held, triangle
+    mask, got, flat, gating, final, proj, out, first, next_gating, held, triangle
 ):
     weights = halved(proj)
     closing = halved(final)
-    mask = masks(lambda n: token_s[n // 128, n % 128], token_v)
     unpack(got, triangle)
     for group in range(2):
         for slot in range(0, 8, 2):
@@ -178,7 +169,7 @@
             lanes = slice(128 * tile, 128 * (tile + 2))
             values = finish(triangle, tile, flat, gating, closing)
             first[:, lanes] = values
-            next_gating[:, lanes] = sides(norm(values, mask(tile)), weights, held, slot)
+            next_gating[:, lanes] = sides(norm(values, mask_of(mask, tile)), weights, held, slot)
         pack(held, out, group)
 
 
@@ -225,19 +216,18 @@
 
     scratch = [
         held,
-        pltpu.SMEM((4, 128), jnp.int32),
         pltpu.VMEM((4, 128), jnp.int32),
-        pltpu.VMEM(pair.shape, F32),
+        pltpu.VMEM((2, 2, 2, 4, 64, 128), F32),
         pltpu.VMEM(out_proj.shape, F32),
-        pltpu.SemaphoreType.DMA((11,)),
+        pltpu.SemaphoreType.DMA((6,)),
     ]
-    sent, flat, gating = call(
-        project_kernel, (message, whole, whole), scratch, [HBM] * 3, 2 * 2048 * 128 * 640
-    )(*[pltpu.with_memory_space_constraint(v, pltpu.HBM) for v in (lines, pair, out_proj)])
+    sent, flat, gating, mask = call(
+        project_kernel, (message, whole, whole, struct((TILES, 128), F32)), scratch, [HBM] * 3, 2 * 2048 * 128 * 640
+    )(*[pltpu.with_memory_space_constraint(v, pltpu.HBM) for v in (lines, pair.reshape(2, 2, 2, 4, 64, 128), out_proj)])
     sums = swap(triangle(swap(sent), 1))
     sent, first, gating = call(
-        middle_kernel, (message, whole, whole), [held, held], [SMEM] + [VMEM] * 6, 2 * 2048 * 128 * 768
-    )(lines, lines, sums, flat, gating, out_final, in_proj)
+        middle_kernel, (message, whole, whole), [held, held], [VMEM] * 6, 2 * 2048 * 128 * 768
+    )(mask, sums, flat, gating, out_final, in_proj)
     sums = swap(triangle(swap(sent), 0))
     return pl.pallas_call(
         last_kernel,

time: 100 us -> 98 us (0.980)
  Pallas kernels: 10.2 us -> 8.49 us
    pallas_call x2, Pallas kernels: 6.64 us -> 4.95 us  [the longest x1 2.75 us: shards(): call(project_kernel, (message, whole, whole, struct((TILES, 128), F32)),...]
where the time goes in v3:
time: 98 us; the launch traced here: 97.7 us
  blocking collectives  89.2 us (91%)
  Pallas kernels  8.49 us (9%)
    all_to_all x4, blocking collectives, swap(): return lax.all_to_all(values, axes, 0, 0, tiled=True)  89.2 us
    pallas_call x1, Pallas kernels, shards(): call(project_kernel, (message, whole, whole, struct((TILES, 128), F32)),...  2.75 us
    pallas_call x1, Pallas kernels, shards(): call(middle_kernel, (message, whole, whole), [held, held], [VMEM] * 6, 2...  2.2 us

profile of v3, /device:TPU:1, one launch (start us, length us, event | category | flops | bytes accessed | tf_op | source)
XLA Modules:
  0.0 97.7 jit_solution(9107341329302553301)
XLA Ops:
  0.0 2.7 %shard_map.64 = (bf16[128,32,128]{2,1,0:T(8,128)(2,1)S(1)}, f32[128,2048]{1,0:T(8,128)S(1)}, f32[128,2048]{1,0:T(8,128)S(1)}, f32[16,128]{1,0:T(8,128)S(1)}) custom-call(s32[4,128]{1,0:T(4,128)} %bitcast.11, f32[2,2,2,4,64,128]{5,4,3,2,1,0:T(8,128)} %bitcast.10, f32[128,640]{1,0:T(8,128)} %proj_h.1), custom_call_target="tpu_custom_call" | custom-call | flops 335544320 | bytes 3145728 | tf_op jit(solution)/shard_map/pallas_call | solution.py:224
  2.8 30.4 %all_to_all.20 = bf16[128,32,128]{2,1,0:T(8,128)(2,1)S(1)} all-to-all(bf16[128,32,128]{2,1,0:T(8,128)(2,1)S(1)} %get-tuple-element.13), channel_id=1, replica_groups=mesh['row'=16,'col'=8] {'row','col'}, dimensions={0} | all-to-all | bytes 2097152 | tf_op jit(solution)/shard_map/all_to_all | solution.py:210
  33.2 1.0 %shard_map.65 = bf16[16,8,16,128]{3,2,1,0:T(8,128)(2,1)S(1)} custom-call(bf16[16,8,32,128]{3,2,1,0:T(8,128)(2,1)S(1)} %bitcast.6), custom_call_target="tpu_custom_call" | custom-call | flops 268435456 | bytes 3145728 | tf_op jit(solution)/shard_map/pallas_call | solution.py:214
  34.2 0.0 copy-start
  34.2 0.0 copy-start.2
  34.3 17.8 %all_to_all.21.got = bf16[128,16,128]{2,1,0:T(8,128)(2,1)S(1)} all-to-all(bf16[128,16,128]{2,1,0:T(8,128)(2,1)S(1)} %bitcast.8), channel_id=1, replica_groups=mesh['row'=16,'col'=8] {'row','col'}, dimensions={0} | all-to-all | bytes 1048576 | tf_op jit(solution)/shard_map/all_to_all | solution.py:210
  52.0 0.0 copy-done
  52.0 0.0 copy-done.2
  52.0 2.2 %shard_map.66 = (bf16[128,32,128]{2,1,0:T(8,128)(2,1)S(1)}, f32[128,2048]{1,0:T(8,128)S(1)}, f32[128,2048]{1,0:T(8,128)S(1)}) custom-call(f32[16,128]{1,0:T(8,128)S(1)} %get-tuple-element.12.mask, bf16[128,16,128]{2,1,0:T(8,128)(2,1)S(1)} %all_to_all.21.got, f32[128,2048]{1,0:T(8,128)S(1)} %get-tuple-element.14.flat, ...), custom_call_target="tpu_custom_call" | custom-call | flops 402653184 | bytes 3145728 | tf_op jit(solution)/shard_map/pallas_call | solution.py:228
  54.2 23.2 %all_to_all.22 = bf16[128,32,128]{2,1,0:T(8,128)(2,1)S(1)} all-to-all(bf16[128,32,128]{2,1,0:T(8,128)(2,1)S(1)} %get-tuple-element.16), channel_id=1, replica_groups=mesh['row'=16,'col'=8] {'row','col'}, dimensions={0} | all-to-all | bytes 2097152 | tf_op jit(solution)/shard_map/all_to_all | solution.py:210
  77.4 0.9 shard_map.67
  78.3 0.0 copy-start.1
  78.3 17.8 %all_to_all.23.got = bf16[128,16,128]{2,1,0:T(8,128)(2,1)S(1)} all-to-all(bf16[128,16,128]{2,1,0:T(8,128)(2,1)S(1)} %bitcast.9), channel_id=1, replica_groups=mesh['row'=16,'col'=8] {'row','col'}, dimensions={0} | all-to-all | bytes 1048576 | tf_op jit(solution)/shard_map/all_to_all | solution.py:210
  96.1 0.0 copy-done.1
  96.1 1.6 %shard_map.68 = f32[32,64,128]{2,1,0:T(8,128)} custom-call(bf16[128,16,128]{2,1,0:T(8,128)(2,1)S(1)} %all_to_all.23.got, f32[128,2048]{1,0:T(8,128)S(1)} %get-tuple-element.17.first, f32[128,2048]{1,0:T(8,128)S(1)} %get-tuple-element.18.gating, f32[128,128]{1,0:T(8,128)S(1)} %copy-done.1), custom_call_target="tpu_custom_call" | custom-call | flops 67108864 | bytes 3145728 | tf_op jit(solution)/shard_map/pallas_call | solution.py:232
Async XLA Ops:
  34.2 17.8 %copy-start = (f32[128,640]{1,0:T(8,128)S(1)}, f32[128,640]{1,0:T(8,128)}, u32[]{:S(2)}) copy-start(f32[128,640]{1,0:T(8,128)} %proj.1) | copy-start | bytes 983044
  34.2 17.8 %copy-start.2 = (f32[128,128]{1,0:T(8,128)S(1)}, f32[128,128]{1,0:T(8,128)}, u32[]{:S(2)}) copy-start(f32[128,128]{1,0:T(8,128)} %final.2) | copy-start | bytes 196612
  78.3 17.8 %copy-start.1 = (f32[128,128]{1,0:T(8,128)S(1)}, f32[128,128]{1,0:T(8,128)}, u32[]{:S(2)}) copy-start(f32[128,128]{1,0:T(8,128)} %final.3) | copy-start | bytes 196612

commit v4 on v3

--- a/solution.py
+++ b/solution.py
@@ -130,14 +130,14 @@
 def triangle_kernel(contract, got, out, left, right):
     operands(got, left, right)
     low = low_lanes((16, 128))
-    for k in range(0, 16, 4):
-        rows = slice(32 * k, 32 * (k + 4))
+    for k in range(0, 16, 16):
+        rows = slice(32 * k, 32 * (k + 16))
         if contract == 1:
             sums = dot(left[rows, :], right[...], ((1,), (1,)))
         else:
             sums = dot(left[:, rows], right[...], ((0,), (0,)))
-        sums = sums.reshape(4, 2, 2, 8, 512)
-        for n in range(4):
+        sums = sums.reshape(16, 2, 2, 8, 512)
+        for n in range(16):
             for m in range(4):
                 lanes = slice(128 * m, 128 * (m + 1))
                 top = sums[n, :, 0, :, lanes].reshape(16, 128)

time: 98 us -> 97.7 us (level)
  no operation moved by 1% of the time
where the time goes in v4:
time: 97.7 us; the launch traced here: 97.4 us
  blocking collectives  89.2 us (91%)
  Pallas kernels  8.17 us (8%)
    all_to_all x4, blocking collectives, swap(): return lax.all_to_all(values, axes, 0, 0, tiled=True)  89.2 us
    pallas_call x1, Pallas kernels, shards(): call(project_kernel, (message, whole, whole, struct((TILES, 128), F32)),...  2.75 us
    pallas_call x1, Pallas kernels, shards(): call(middle_kernel, (message, whole, whole), [held, held], [VMEM] * 6, 2...  2.2 us

profile of v4, /device:TPU:1, one launch (start us, length us, event | category | flops | bytes accessed | tf_op | source)
XLA Modules:
  0.0 97.4 jit_solution(11693317293389469676)
XLA Ops:
  0.0 2.7 %shard_map.64 = (bf16[128,32,128]{2,1,0:T(8,128)(2,1)S(1)}, f32[128,2048]{1,0:T(8,128)S(1)}, f32[128,2048]{1,0:T(8,128)S(1)}, f32[16,128]{1,0:T(8,128)S(1)}) custom-call(s32[4,128]{1,0:T(4,128)} %bitcast.11, f32[2,2,2,4,64,128]{5,4,3,2,1,0:T(8,128)} %bitcast.10, f32[128,640]{1,0:T(8,128)} %proj_h.1), custom_call_target="tpu_custom_call" | custom-call | flops 335544320 | bytes 3145728 | tf_op jit(solution)/shard_map/pallas_call | solution.py:224
  2.8 30.4 %all_to_all.20 = bf16[128,32,128]{2,1,0:T(8,128)(2,1)S(1)} all-to-all(bf16[128,32,128]{2,1,0:T(8,128)(2,1)S(1)} %get-tuple-element.13), channel_id=1, replica_groups=mesh['row'=16,'col'=8] {'row','col'}, dimensions={0} | all-to-all | bytes 2097152 | tf_op jit(solution)/shard_map/all_to_all | solution.py:210
  33.2 0.7 shard_map.65
  33.9 0.0 copy-start
  33.9 0.0 copy-start.2
  33.9 17.8 %all_to_all.21.got = bf16[128,16,128]{2,1,0:T(8,128)(2,1)S(1)} all-to-all(bf16[128,16,128]{2,1,0:T(8,128)(2,1)S(1)} %bitcast.8), channel_id=1, replica_groups=mesh['row'=16,'col'=8] {'row','col'}, dimensions={0} | all-to-all | bytes 1048576 | tf_op jit(solution)/shard_map/all_to_all | solution.py:210
  51.7 0.0 copy-done
  51.7 0.0 copy-done.2
  51.7 2.2 %shard_map.66 = (bf16[128,32,128]{2,1,0:T(8,128)(2,1)S(1)}, f32[128,2048]{1,0:T(8,128)S(1)}, f32[128,2048]{1,0:T(8,128)S(1)}) custom-call(f32[16,128]{1,0:T(8,128)S(1)} %get-tuple-element.12.mask, bf16[128,16,128]{2,1,0:T(8,128)(2,1)S(1)} %all_to_all.21.got, f32[128,2048]{1,0:T(8,128)S(1)} %get-tuple-element.14.flat, ...), custom_call_target="tpu_custom_call" | custom-call | flops 402653184 | bytes 3145728 | tf_op jit(solution)/shard_map/pallas_call | solution.py:228
  53.9 23.2 %all_to_all.22 = bf16[128,32,128]{2,1,0:T(8,128)(2,1)S(1)} all-to-all(bf16[128,32,128]{2,1,0:T(8,128)(2,1)S(1)} %get-tuple-element.16), channel_id=1, replica_groups=mesh['row'=16,'col'=8] {'row','col'}, dimensions={0} | all-to-all | bytes 2097152 | tf_op jit(solution)/shard_map/all_to_all | solution.py:210
  77.1 0.9 shard_map.67
  78.0 0.0 copy-start.1
  78.0 17.8 %all_to_all.23.got = bf16[128,16,128]{2,1,0:T(8,128)(2,1)S(1)} all-to-all(bf16[128,16,128]{2,1,0:T(8,128)(2,1)S(1)} %bitcast.9), channel_id=1, replica_groups=mesh['row'=16,'col'=8] {'row','col'}, dimensions={0} | all-to-all | bytes 1048576 | tf_op jit(solution)/shard_map/all_to_all | solution.py:210
  95.8 0.0 copy-done.1
  95.8 1.6 %shard_map.68 = f32[32,64,128]{2,1,0:T(8,128)} custom-call(bf16[128,16,128]{2,1,0:T(8,128)(2,1)S(1)} %all_to_all.23.got, f32[128,2048]{1,0:T(8,128)S(1)} %get-tuple-element.17.first, f32[128,2048]{1,0:T(8,128)S(1)} %get-tuple-element.18.gating, f32[128,128]{1,0:T(8,128)S(1)} %copy-done.1), custom_call_target="tpu_custom_call" | custom-call | flops 67108864 | bytes 3145728 | tf_op jit(solution)/shard_map/pallas_call | solution.py:232
Async XLA Ops:
  33.9 17.8 %copy-start = (f32[128,640]{1,0:T(8,128)S(1)}, f32[128,640]{1,0:T(8,128)}, u32[]{:S(2)}) copy-start(f32[128,640]{1,0:T(8,128)} %proj.1) | copy-start | bytes 983044
  33.9 17.8 %copy-start.2 = (f32[128,128]{1,0:T(8,128)S(1)}, f32[128,128]{1,0:T(8,128)}, u32[]{:S(2)}) copy-start(f32[128,128]{1,0:T(8,128)} %final.2) | copy-start | bytes 196612
  78.0 17.8 %copy-start.1 = (f32[128,128]{1,0:T(8,128)S(1)}, f32[128,128]{1,0:T(8,128)}, u32[]{:S(2)}) copy-start(f32[128,128]{1,0:T(8,128)} %final.3) | copy-start | bytes 196612

commit v5 on v4

--- a/solution.py
+++ b/solution.py
@@ -163,13 +163,13 @@
     weights = halved(proj)
     closing = halved(final)
     unpack(got, triangle)
+    for tile in range(0, TILES, 2):
+        first[:, 128 * tile : 128 * (tile + 2)] = finish(triangle, tile, flat, gating, closing)
     for group in range(2):
         for slot in range(0, 8, 2):
             tile = 8 * group + slot
             lanes = slice(128 * tile, 128 * (tile + 2))
-            values = finish(triangle, tile, flat, gating, closing)
-            first[:, lanes] = values
-            next_gating[:, lanes] = sides(norm(values, mask_of(mask, tile)), weights, held, slot)
+            next_gating[:, lanes] = sides(norm(first[:, lanes], mask_of(mask, tile)), weights, held, slot)
         pack(held, out, group)
 
 

time: 97.7 us -> 97.3 us (level)
  no operation moved by 1% of the time
where the time goes in v5:
time: 97.3 us; the launch traced here: 97 us
  blocking collectives  89.2 us (92%)
  Pallas kernels  7.81 us (8%)
    all_to_all x4, blocking collectives, swap(): return lax.all_to_all(values, axes, 0, 0, tiled=True)  89.2 us
    pallas_call x1, Pallas kernels, shards(): call(project_kernel, (message, whole, whole, struct((TILES, 128), F32)),...  2.75 us

profile of v5, /device:TPU:1, one launch (start us, length us, event | category | flops | bytes accessed | tf_op | source)
XLA Modules:
  0.0 97.0 jit_solution(7548906682174509634)
XLA Ops:
  0.0 2.7 %shard_map.64 = (bf16[128,32,128]{2,1,0:T(8,128)(2,1)S(1)}, f32[128,2048]{1,0:T(8,128)S(1)}, f32[128,2048]{1,0:T(8,128)S(1)}, f32[16,128]{1,0:T(8,128)S(1)}) custom-call(s32[4,128]{1,0:T(4,128)} %bitcast.11, f32[2,2,2,4,64,128]{5,4,3,2,1,0:T(8,128)} %bitcast.10, f32[128,640]{1,0:T(8,128)} %proj_h.1), custom_call_target="tpu_custom_call" | custom-call | flops 335544320 | bytes 3145728 | tf_op jit(solution)/shard_map/pallas_call | solution.py:224
  2.8 30.4 %all_to_all.20 = bf16[128,32,128]{2,1,0:T(8,128)(2,1)S(1)} all-to-all(bf16[128,32,128]{2,1,0:T(8,128)(2,1)S(1)} %get-tuple-element.13), channel_id=1, replica_groups=mesh['row'=16,'col'=8] {'row','col'}, dimensions={0} | all-to-all | bytes 2097152 | tf_op jit(solution)/shard_map/all_to_all | solution.py:210
  33.2 0.7 shard_map.65
  33.9 0.0 copy-start
  33.9 0.0 copy-start.2
  33.9 17.8 %all_to_all.21.got = bf16[128,16,128]{2,1,0:T(8,128)(2,1)S(1)} all-to-all(bf16[128,16,128]{2,1,0:T(8,128)(2,1)S(1)} %bitcast.8), channel_id=1, replica_groups=mesh['row'=16,'col'=8] {'row','col'}, dimensions={0} | all-to-all | bytes 1048576 | tf_op jit(solution)/shard_map/all_to_all | solution.py:210
  51.7 0.0 copy-done
  51.7 0.0 copy-done.2
  51.7 1.8 %shard_map.66 = (bf16[128,32,128]{2,1,0:T(8,128)(2,1)S(1)}, f32[128,2048]{1,0:T(8,128)S(1)}, f32[128,2048]{1,0:T(8,128)S(1)}) custom-call(f32[16,128]{1,0:T(8,128)S(1)} %get-tuple-element.12.mask, bf16[128,16,128]{2,1,0:T(8,128)(2,1)S(1)} %all_to_all.21.got, f32[128,2048]{1,0:T(8,128)S(1)} %get-tuple-element.14.flat, ...), custom_call_target="tpu_custom_call" | custom-call | flops 402653184 | bytes 3145728 | tf_op jit(solution)/shard_map/pallas_call | solution.py:228
  53.5 23.2 %all_to_all.22 = bf16[128,32,128]{2,1,0:T(8,128)(2,1)S(1)} all-to-all(bf16[128,32,128]{2,1,0:T(8,128)(2,1)S(1)} %get-tuple-element.16), channel_id=1, replica_groups=mesh['row'=16,'col'=8] {'row','col'}, dimensions={0} | all-to-all | bytes 2097152 | tf_op jit(solution)/shard_map/all_to_all | solution.py:210
  76.8 0.9 shard_map.67
  77.6 0.0 copy-start.1
  77.6 17.8 %all_to_all.23.got = bf16[128,16,128]{2,1,0:T(8,128)(2,1)S(1)} all-to-all(bf16[128,16,128]{2,1,0:T(8,128)(2,1)S(1)} %bitcast.9), channel_id=1, replica_groups=mesh['row'=16,'col'=8] {'row','col'}, dimensions={0} | all-to-all | bytes 1048576 | tf_op jit(solution)/shard_map/all_to_all | solution.py:210
  95.4 0.0 copy-done.1
  95.4 1.6 %shard_map.68 = f32[32,64,128]{2,1,0:T(8,128)} custom-call(bf16[128,16,128]{2,1,0:T(8,128)(2,1)S(1)} %all_to_all.23.got, f32[128,2048]{1,0:T(8,128)S(1)} %get-tuple-element.17.first, f32[128,2048]{1,0:T(8,128)S(1)} %get-tuple-element.18.gating, f32[128,128]{1,0:T(8,128)S(1)} %copy-done.1), custom_call_target="tpu_custom_call" | custom-call | flops 67108864 | bytes 3145728 | tf_op jit(solution)/shard_map/pallas_call | solution.py:232
Async XLA Ops:
  33.9 17.8 %copy-start = (f32[128,640]{1,0:T(8,128)S(1)}, f32[128,640]{1,0:T(8,128)}, u32[]{:S(2)}) copy-start(f32[128,640]{1,0:T(8,128)} %proj.1) | copy-start | bytes 983044
  33.9 17.8 %copy-start.2 = (f32[128,128]{1,0:T(8,128)S(1)}, f32[128,128]{1,0:T(8,128)}, u32[]{:S(2)}) copy-start(f32[128,128]{1,0:T(8,128)} %final.2) | copy-start | bytes 196612
  77.6 17.8 %copy-start.1 = (f32[128,128]{1,0:T(8,128)S(1)}, f32[128,128]{1,0:T(8,128)}, u32[]{:S(2)}) copy-start(f32[128,128]{1,0:T(8,128)} %final.3) | copy-start | bytes 196612

commit v6 on v5

v6 whole, which is shorter than its diff:
```python
import functools

import jax
import jax.numpy as jnp
from jax import lax
from jax.experimental import pallas as pl
from jax.experimental.pallas import tpu as pltpu
from jax.sharding import PartitionSpec as P

HALF = 64
TILES = 16
F32 = jnp.float32
BF16 = jnp.bfloat16
VMEM = pl.BlockSpec(memory_space=pltpu.VMEM)
SMEM = pl.BlockSpec(memory_space=pltpu.SMEM)
HBM = pl.BlockSpec(memory_space=pltpu.HBM)


def call(kernel, outs, scratch, specs, flops, limit=16):
    return pl.pallas_call(
        kernel,
        out_shape=outs,
        in_specs=specs,
        out_specs=jax.tree.map(lambda _: VMEM, outs),
        scratch_shapes=scratch,
        compiler_params=pltpu.CompilerParams(vmem_limit_bytes=limit * 1024 * 1024),
        cost_estimate=pl.CostEstimate(flops=flops, bytes_accessed=3 << 20, transcendentals=1 << 19),
    )


def low_lanes(shape):
    return lax.broadcasted_iota(jnp.int32, shape, len(shape) - 1) < HALF


def turn(values):
    return pltpu.roll(values, HALF, axis=values.ndim - 1)


def norm(values, mask=None):
    scale = 1.0 / values.shape[0]
    centred = values - jnp.sum(values, axis=0, keepdims=True) * scale
    factor = lax.rsqrt(jnp.sum(centred * centred, axis=0, keepdims=True) * scale + 1e-05)
    return centred * (factor if mask is None else factor * mask)


def dot(left, right, dims=((1,), (0,))):
    return lax.dot_general(left, right, (dims, ((), ())), preferred_element_type=F32)


def split(values):
    high = values.astype(BF16)
    return high, (values - high.astype(F32)).astype(BF16)


def halved(weights):
    order = (0, 256, 128, 384, 512) if weights.shape[1] == 640 else (0,)
    parts = [weights[:, k : k + 128].T for k in order]
    high, low = split(jnp.concatenate(parts, axis=0) * 0.5)
    return jnp.concatenate([high, high, low], axis=1)


def masks(tokens):
    row = lax.axis_index("row")
    col = lax.axis_index("col")
    line = tokens[pl.ds(col // 2, 1), :].astype(F32)
    pick = jnp.where(low_lanes((1, 128)), 1, 0) != col % 2
    cols = jnp.where(pick, line, turn(line))
    line = jnp.broadcast_to(tokens[pl.ds(row // 4, 1), :].astype(F32), (32, 128))
    lane = lax.broadcasted_iota(jnp.int32, (32, 128), 1)
    own = lax.broadcasted_iota(jnp.int32, (32, 128), 0) + 32 * (row % 4)
    rows = jnp.sum(jnp.where(lane == own, line, 0.0), axis=1, keepdims=True) * cols
    return jnp.where(low_lanes((TILES, 128)), rows[:TILES], rows[TILES:])


def mask_of(mask, tile):
    return jnp.concatenate([mask[tile : tile + 1], mask[tile + 1 : tile + 2]], axis=1)


def pair_tile(pair, tile):
    return pair[:, tile].reshape(128, 128).T


def three(weights, values):
    high, low = split(values)
    return dot(weights, jnp.concatenate([high, low, high], axis=0))


def sides(normed, weights, held, tile):
    high, low = split(normed)
    both = jnp.concatenate([high, low], axis=0)
    gates = dot(weights[256:, :256], both)
    sided = dot(weights[:256, :256], both) + dot(weights[:256, 256:], high)
    left = ((1.0 + jnp.tanh(gates[:128])) * sided[:128]).astype(BF16)
    right = ((1.0 + jnp.tanh(gates[128:256])) * sided[128:]).astype(BF16)
    for k in range(2):
        lanes = slice(128 * k, 128 * (k + 1))
        held[0, tile + k] = left[:, lanes]
        held[1, tile + k] = right[:, lanes]
    return 1.0 + jnp.tanh(gates[256:])


def pack(held, out):
    for side in range(2):
        for k in range(0, 128, 32):
            out[k : k + 32, 16 * side : 16 * side + 16, :] = jnp.swapaxes(held[side, :, k : k + 32, :], 0, 1)


def project_kernel(token_h, pair_h, proj_h, out, flat, gating, mask, held, tokens, pair, proj, semaphores):
    parts = [(slice(None), pl.ds(4 * k, 4)) for k in range(4)]
    copies = [
        pltpu.make_async_copy(pair_h.at[part], pair.at[part], semaphores.at[k])
        for k, part in enumerate(parts)
    ]
    weight_copy = pltpu.make_async_copy(proj_h, proj, semaphores.at[4])
    token_copy = pltpu.make_async_copy(token_h, tokens, semaphores.at[5])
    for copy in [weight_copy, token_copy] + copies:
        copy.start()
    for copy in copies:
        copy.wait()
    weight_copy.wait()
    token_copy.wait()
    weights = halved(proj)
    mask[...] = masks(tokens)
    for tile in range(0, TILES, 2):
        lanes = slice(128 * tile, 128 * (tile + 2))
        values = jnp.concatenate([pair_tile(pair, tile), pair_tile(pair, tile + 1)], axis=1)
        flat[:, lanes] = values
        gating[:, lanes] = sides(norm(values, mask_of(mask, tile)), weights, held, tile)
    pack(held, out)


def operands(got, left, right):
    for side, matrix in enumerate((left, right)):
        for k in range(4):
            lanes = slice(128 * k, 128 * (k + 1))
            even = got[:, 2 * k, 16 * side : 16 * side + 16]
            odd = got[:, 2 * k + 1, 16 * side : 16 * side + 16]
            matrix[:, 0, :, lanes] = jnp.concatenate([even[..., :HALF], odd[..., :HALF]], axis=2)
            matrix[:, 1, :, lanes] = jnp.concatenate([even[..., HALF:], odd[..., HALF:]], axis=2)
    return left[...].reshape(512, 512), right[...].reshape(512, 512)


def triangle_kernel(contract, got, out, left, right):
    left, right = operands(got, left, right)
    sums = dot(left, right, ((contract,), (contract,))).reshape(16, 2, 16, 512)
    low = low_lanes((16, 128))
    for n in range(16):
        for m in range(4):
            lanes = slice(128 * m, 128 * (m + 1))
            top, bottom = sums[n, 0, :, lanes], sums[n, 1, :, lanes]
            out[n, 2 * m] = jnp.where(low, top, turn(bottom)).astype(BF16)
            out[n, 2 * m + 1] = jnp.where(low, turn(top), bottom).astype(BF16)


def unpack(got, triangle):
    for k in range(0, 128, 32):
        triangle[:, k : k + 32, :] = jnp.swapaxes(got[k : k + 32], 0, 1)


def finish(triangle, tile, flat, gating, closing):
    lanes = slice(128 * tile, 128 * (tile + 2))
    sums = jnp.concatenate([triangle[tile], triangle[tile + 1]], axis=1).astype(F32)
    return flat[:, lanes] + gating[:, lanes] * three(closing, norm(sums))


def middle_kernel(
    mask, got, flat, gating, final, proj, out, first, next_gating, held, triangle
):
    weights = halved(proj)
    closing = halved(final)
    unpack(got, triangle)
    for tile in range(0, TILES, 2):
        first[:, 128 * tile : 128 * (tile + 2)] = finish(triangle, tile, flat, gating, closing)
    for tile in range(0, TILES, 2):
        lanes = slice(128 * tile, 128 * (tile + 2))
        next_gating[:, lanes] = sides(norm(first[:, lanes], mask_of(mask, tile)), weights, held, tile)
    pack(held, out)


def last_kernel(got, first, gating, final, out, triangle, done, semaphores):
    closing = halved(final)
    unpack(got, triangle)
    copies = []
    for tile in range(0, TILES, 2):
        values = finish(triangle, tile, first, gating, closing)
        for k in range(2):
            part = values[:, 128 * k : 128 * (k + 1)].T
            done[tile + k] = part[:HALF]
            done[tile + k + 16] = part[HALF:]
        if tile % 4 == 2:
            for start in (tile - 2, tile + 14):
                rows = pl.ds(start, 4)
                copies.append(pltpu.make_async_copy(done.at[rows], out.at[rows], semaphores.at[len(copies)]))
                copies[-1].start()
    for copy in copies:
        copy.wait()


def shards(pair, token_mask, out_proj, out_final, in_proj, in_final):
    axes = ("row", "col")
    struct = jax.ShapeDtypeStruct
    lines = token_mask.reshape(4, 128)
    message = struct((128, 32, 128), BF16)
    answer = struct((16, 8, 16, 128), BF16)
    whole = struct((128, 2048), F32)
    held = pltpu.VMEM((2, TILES, 128, 128), BF16)
    sums_held = pltpu.VMEM((TILES, 128, 128), BF16)
    operand = pltpu.VMEM((16, 2, 16, 512), BF16)

    def swap(values):
        return lax.all_to_all(values, axes, 0, 0, tiled=True)

    def triangle(got, contract):
        kernel = functools.partial(triangle_kernel, contract)
        sums = call(kernel, answer, [operand, operand], [VMEM], 2 * 512**3)(got.reshape(16, 8, 32, 128))
        return sums.reshape(128, 16, 128)

    scratch = [
        held,
        pltpu.VMEM((4, 128), jnp.int32),
        pltpu.VMEM((2, TILES, HALF, 128), F32),
        pltpu.VMEM(out_proj.shape, F32),
        pltpu.SemaphoreType.DMA((6,)),
    ]
    sent, flat, gating, mask = call(
        project_kernel, (message, whole, whole, struct((TILES, 128), F32)), scratch, [HBM] * 3, 2 * 2048 * 128 * 640
    )(*[pltpu.with_memory_space_constraint(v, pltpu.HBM) for v in (lines, pair.reshape(2, TILES, HALF, 128), out_proj)])
    sums = swap(triangle(swap(sent), 1))
    sent, first, gating = call(
        middle_kernel, (message, whole, whole), [held, sums_held], [VMEM] * 6, 2 * 2048 * 128 * 768
    )(mask, sums, flat, gating, out_final, in_proj)
    sums = swap(triangle(swap(sent), 0))
    return pl.pallas_call(
        last_kernel,
        out_shape=struct(pair.shape, F32),
        in_specs=[VMEM] * 4,
        out_specs=HBM,
        scratch_shapes=[sums_held, pltpu.VMEM(pair.shape, F32), pltpu.SemaphoreType.DMA((8,))],
        compiler_params=pltpu.CompilerParams(vmem_limit_bytes=16 * 1024 * 1024),
        cost_estimate=pl.CostEstimate(flops=2 * 2048 * 128 * 128, bytes_accessed=3 << 20, transcendentals=0),
    )(sums, first, gating, in_final)


def solution(mesh):
    placed = (P("row", "col", None), P(), P(), P(), P(), P())
    return jax.shard_map(
        shards, mesh=mesh, in_specs=placed, out_specs=P("row", "col", None), check_vma=False
    )
```

time: 97.3 us -> 98 us (level)
  no operation moved by 1% of the time
where the time goes in v6:
time: 98 us; the launch traced here: 97.7 us
  blocking collectives  89.2 us (91%)
  Pallas kernels  8.5 us (9%)
    all_to_all x4, blocking collectives, swap(): return lax.all_to_all(values, axes, 0, 0, tiled=True)  89.2 us
    pallas_call x1, Pallas kernels, shards(): call(project_kernel, (message, whole, whole, struct((TILES, 128), F32)),...  2.96 us
    pallas_call x1, Pallas kernels, shards(): call(middle_kernel, (message, whole, whole), [held, sums_held], [VMEM] *...  2.25 us

profile of v6, /device:TPU:1, one launch (start us, length us, event | category | flops | bytes accessed | tf_op | source)
XLA Modules:
  0.0 97.7 jit_solution(10454548074871397152)
XLA Ops:
  0.0 3.0 %shard_map.64 = (bf16[128,32,128]{2,1,0:T(8,128)(2,1)S(1)}, f32[128,2048]{1,0:T(8,128)S(1)}, f32[128,2048]{1,0:T(8,128)S(1)}, f32[16,128]{1,0:T(8,128)S(1)}) custom-call(s32[4,128]{1,0:T(4,128)} %bitcast.11, f32[2,16,64,128]{3,2,1,0:T(8,128)} %bitcast.10, f32[128,640]{1,0:T(8,128)} %proj_h.1), custom_call_target="tpu_custom_call" | custom-call | flops 335544320 | bytes 3145728 | tf_op jit(solution)/shard_map/pallas_call | solution.py:225
  3.0 30.4 %all_to_all.20 = bf16[128,32,128]{2,1,0:T(8,128)(2,1)S(1)} all-to-all(bf16[128,32,128]{2,1,0:T(8,128)(2,1)S(1)} %get-tuple-element.13), channel_id=1, replica_groups=mesh['row'=16,'col'=8] {'row','col'}, dimensions={0} | all-to-all | bytes 2097152 | tf_op jit(solution)/shard_map/all_to_all | solution.py:211
  33.4 0.7 shard_map.65
  34.1 0.0 copy-start
  34.2 0.0 copy-start.2
  34.2 17.8 %all_to_all.21.got = bf16[128,16,128]{2,1,0:T(8,128)(2,1)S(1)} all-to-all(bf16[128,16,128]{2,1,0:T(8,128)(2,1)S(1)} %bitcast.8), channel_id=1, replica_groups=mesh['row'=16,'col'=8] {'row','col'}, dimensions={0} | all-to-all | bytes 1048576 | tf_op jit(solution)/shard_map/all_to_all | solution.py:211
  51.9 0.0 copy-done
  51.9 0.0 copy-done.2
  51.9 2.2 %shard_map.66 = (bf16[128,32,128]{2,1,0:T(8,128)(2,1)S(1)}, f32[128,2048]{1,0:T(8,128)S(1)}, f32[128,2048]{1,0:T(8,128)S(1)}) custom-call(f32[16,128]{1,0:T(8,128)S(1)} %get-tuple-element.12.mask, bf16[128,16,128]{2,1,0:T(8,128)(2,1)S(1)} %all_to_all.21.got, f32[128,2048]{1,0:T(8,128)S(1)} %get-tuple-element.14.flat, ...), custom_call_target="tpu_custom_call" | custom-call | flops 402653184 | bytes 3145728 | tf_op jit(solution)/shard_map/pallas_call | solution.py:229
  54.2 23.2 %all_to_all.22 = bf16[128,32,128]{2,1,0:T(8,128)(2,1)S(1)} all-to-all(bf16[128,32,128]{2,1,0:T(8,128)(2,1)S(1)} %get-tuple-element.16), channel_id=1, replica_groups=mesh['row'=16,'col'=8] {'row','col'}, dimensions={0} | all-to-all | bytes 2097152 | tf_op jit(solution)/shard_map/all_to_all | solution.py:211
  77.4 0.8 shard_map.67
  78.2 0.0 copy-start.1
  78.2 17.8 %all_to_all.23.got = bf16[128,16,128]{2,1,0:T(8,128)(2,1)S(1)} all-to-all(bf16[128,16,128]{2,1,0:T(8,128)(2,1)S(1)} %bitcast.9), channel_id=1, replica_groups=mesh['row'=16,'col'=8] {'row','col'}, dimensions={0} | all-to-all | bytes 1048576 | tf_op jit(solution)/shard_map/all_to_all | solution.py:211
  96.0 0.0 copy-done.1
  96.0 1.7 %shard_map.68 = f32[32,64,128]{2,1,0:T(8,128)} custom-call(bf16[128,16,128]{2,1,0:T(8,128)(2,1)S(1)} %all_to_all.23.got, f32[128,2048]{1,0:T(8,128)S(1)} %get-tuple-element.17.first, f32[128,2048]{1,0:T(8,128)S(1)} %get-tuple-element.18.gating, f32[128,128]{1,0:T(8,128)S(1)} %copy-done.1), custom_call_target="tpu_custom_call" | custom-call | flops 67108864 | bytes 3145728 | tf_op jit(solution)/shard_map/pallas_call | solution.py:233
Async XLA Ops:
  34.1 17.8 %copy-start = (f32[128,640]{1,0:T(8,128)S(1)}, f32[128,640]{1,0:T(8,128)}, u32[]{:S(2)}) copy-start(f32[128,640]{1,0:T(8,128)} %proj.1) | copy-start | bytes 983044
  34.2 17.8 %copy-start.2 = (f32[128,128]{1,0:T(8,128)S(1)}, f32[128,128]{1,0:T(8,128)}, u32[]{:S(2)}) copy-start(f32[128,128]{1,0:T(8,128)} %final.2) | copy-start | bytes 196612
  78.2 17.8 %copy-start.1 = (f32[128,128]{1,0:T(8,128)S(1)}, f32[128,128]{1,0:T(8,128)}, u32[]{:S(2)}) copy-start(f32[128,128]{1,0:T(8,128)} %final.3) | copy-start | bytes 196612

commit v7 on v6

--- a/solution.py
+++ b/solution.py
@@ -53,10 +53,13 @@
 
 
 def halved(weights):
-    order = (0, 256, 128, 384, 512) if weights.shape[1] == 640 else (0,)
-    parts = [weights[:, k : k + 128].T for k in order]
-    high, low = split(jnp.concatenate(parts, axis=0) * 0.5)
-    return jnp.concatenate([high, high, low], axis=1)
+    rows = []
+    for k in range(0, weights.shape[1], 128):
+        high, low = split(weights[:, k : k + 128].T * 0.5)
+        rows.append([jnp.concatenate([high, high], axis=1), jnp.concatenate([low, jnp.zeros_like(low)], axis=1)])
+    if len(rows) == 1:
+        return jnp.concatenate(rows[0], axis=0)
+    return jnp.concatenate(rows[0] + rows[1][:1] + rows[2] + rows[3][:1] + rows[4][:1], axis=0)
 
 
 def masks(tokens):
@@ -80,32 +83,28 @@
     return pair[:, tile].reshape(128, 128).T
 
 
-def three(weights, values):
-    high, low = split(values)
-    return dot(weights, jnp.concatenate([high, low, high], axis=0))
-
-
 def sides(normed, weights, held, tile):
-    high, low = split(normed)
-    both = jnp.concatenate([high, low], axis=0)
-    gates = dot(weights[256:, :256], both)
-    sided = dot(weights[:256, :256], both) + dot(weights[:256, 256:], high)
-    left = ((1.0 + jnp.tanh(gates[:128])) * sided[:128]).astype(BF16)
-    right = ((1.0 + jnp.tanh(gates[128:256])) * sided[128:]).astype(BF16)
-    for k in range(2):
-        lanes = slice(128 * k, 128 * (k + 1))
-        held[0, tile + k] = left[:, lanes]
-        held[1, tile + k] = right[:, lanes]
-    return 1.0 + jnp.tanh(gates[256:])
+    both = jnp.concatenate(split(normed), axis=0)
+
+    def side(k):
+        linear = dot(weights[384 * k : 384 * (k + 1)], both)
+        value = linear[:128] + linear[128:256]
+        value = value + jnp.tanh(linear[256:]) * value
+        for n in range(2):
+            held[k, tile + n] = value[:, 128 * n : 128 * (n + 1)]
+
+    side(0)
+    side(1)
+    return 1.0 + jnp.tanh(dot(weights[768:], both))
 
 
 def pack(held, out):
     for side in range(2):
         for k in range(0, 128, 32):
-            out[k : k + 32, 16 * side : 16 * side + 16, :] = jnp.swapaxes(held[side, :, k : k + 32, :], 0, 1)
-
-
-def project_kernel(token_h, pair_h, proj_h, out, flat, gating, mask, held, tokens, pair, proj, semaphores):
+            out[k : k + 32, 16 * side : 16 * side + 16, :] = jnp.swapaxes(held[side, :, k : k + 32, :], 0, 1).astype(BF16)
+
+
+def project_kernel(token_h, pair_h, proj_h, out, flat, gating, mask, held, normed, tokens, pair, proj, semaphores):
     parts = [(slice(None), pl.ds(4 * k, 4)) for k in range(4)]
     copies = [
         pltpu.make_async_copy(pair_h.at[part], pair.at[part], semaphores.at[k])
@@ -113,35 +112,41 @@
     ]
     weight_copy = pltpu.make_async_copy(proj_h, proj, semaphores.at[4])
     token_copy = pltpu.make_async_copy(token_h, tokens, semaphores.at[5])
-    for copy in [weight_copy, token_copy] + copies:
+    for copy in [token_copy] + copies[:2] + [weight_copy] + copies[2:]:
         copy.start()
-    for copy in copies:
-        copy.wait()
-    weight_copy.wait()
     token_copy.wait()
-    weights = halved(proj)
+    copies[0].wait()
+    copies[1].wait()
     mask[...] = masks(tokens)
     for tile in range(0, TILES, 2):
+        if tile == 8:
+            weight_copy.wait()
+            copies[2].wait()
+            copies[3].wait()
+            weights = halved(proj)
         lanes = slice(128 * tile, 128 * (tile + 2))
         values = jnp.concatenate([pair_tile(pair, tile), pair_tile(pair, tile + 1)], axis=1)
         flat[:, lanes] = values
-        gating[:, lanes] = sides(norm(values, mask_of(mask, tile)), weights, held, tile)
+        normed[:, lanes] = norm(values, mask_of(mask, tile))
+    for tile in range(0, TILES, 2):
+        lanes = slice(128 * tile, 128 * (tile + 2))
+        gating[:, lanes] = sides(normed[:, lanes], weights, held, tile)
     pack(held, out)
 
 
-def operands(got, left, right):
-    for side, matrix in enumerate((left, right)):
-        for k in range(4):
-            lanes = slice(128 * k, 128 * (k + 1))
-            even = got[:, 2 * k, 16 * side : 16 * side + 16]
-            odd = got[:, 2 * k + 1, 16 * side : 16 * side + 16]
-            matrix[:, 0, :, lanes] = jnp.concatenate([even[..., :HALF], odd[..., :HALF]], axis=2)
-            matrix[:, 1, :, lanes] = jnp.concatenate([even[..., HALF:], odd[..., HALF:]], axis=2)
-    return left[...].reshape(512, 512), right[...].reshape(512, 512)
-
-
-def triangle_kernel(contract, got, out, left, right):
-    left, right = operands(got, left, right)
+def operands(got):
+    matrices = []
+    for side in range(2):
+        halves = []
+        for lanes in (slice(0, HALF), slice(HALF, 128)):
+            parts = [got[:, k, 16 * side : 16 * side + 16, lanes] for k in range(8)]
+            halves.append(jnp.concatenate(parts, axis=2))
+        matrices.append(jnp.stack(halves, axis=1).reshape(512, 512))
+    return matrices
+
+
+def triangle_kernel(contract, got, out):
+    left, right = operands(got)
     sums = dot(left, right, ((contract,), (contract,))).reshape(16, 2, 16, 512)
     low = low_lanes((16, 128))
     for n in range(16):
@@ -160,7 +165,9 @@
 def finish(triangle, tile, flat, gating, closing):
     lanes = slice(128 * tile, 128 * (tile + 2))
     sums = jnp.concatenate([triangle[tile], triangle[tile + 1]], axis=1).astype(F32)
-    return flat[:, lanes] + gating[:, lanes] * three(closing, norm(sums))
+    product = dot(closing, jnp.concatenate(split(norm(sums)), axis=0))
+    product = product[:128] + product[128:]
+    return flat[:, lanes] + gating[:, lanes] * product
 
 
 def middle_kernel(
@@ -203,20 +210,20 @@
     message = struct((128, 32, 128), BF16)
     answer = struct((16, 8, 16, 128), BF16)
     whole = struct((128, 2048), F32)
-    held = pltpu.VMEM((2, TILES, 128, 128), BF16)
+    held = pltpu.VMEM((2, TILES, 128, 128), F32)
     sums_held = pltpu.VMEM((TILES, 128, 128), BF16)
-    operand = pltpu.VMEM((16, 2, 16, 512), BF16)
 
     def swap(values):
         return lax.all_to_all(values, axes, 0, 0, tiled=True)
 
     def triangle(got, contract):
         kernel = functools.partial(triangle_kernel, contract)
-        sums = call(kernel, answer, [operand, operand], [VMEM], 2 * 512**3)(got.reshape(16, 8, 32, 128))
+        sums = call(kernel, answer, [], [VMEM], 2 * 512**3)(got.reshape(16, 8, 32, 128))
         return sums.reshape(128, 16, 128)
 
     scratch = [
         held,
+        pltpu.VMEM((128, 2048), F32),
         pltpu.VMEM((4, 128), jnp.int32),
         pltpu.VMEM((2, TILES, HALF, 128), F32),
         pltpu.VMEM(out_proj.shape, F32),

time: 98 us -> 97.7 us (level)
  no operation moved by 1% of the time
where the time goes in v7:
time: 97.7 us; the launch traced here: 97.5 us
  blocking collectives  89.2 us (91%)
  Pallas kernels  8.23 us (8%)
    all_to_all x4, blocking collectives, swap(): return lax.all_to_all(values, axes, 0, 0, tiled=True)  89.2 us
    pallas_call x1, Pallas kernels, shards(): call(project_kernel, (message, whole, whole, struct((TILES, 128), F32)),...  2.9 us
    pallas_call x1, Pallas kernels, shards(): call(middle_kernel, (message, whole, whole), [held, sums_held], [VMEM] *...  2.14 us

profile of v7, /device:TPU:1, one launch (start us, length us, event | category | flops | bytes accessed | tf_op | source)
XLA Modules:
  0.0 97.5 jit_solution(17135424247634931936)
XLA Ops:
  0.0 2.9 %shard_map.64 = (bf16[128,32,128]{2,1,0:T(8,128)(2,1)S(1)}, f32[128,2048]{1,0:T(8,128)S(1)}, f32[128,2048]{1,0:T(8,128)S(1)}, f32[16,128]{1,0:T(8,128)S(1)}) custom-call(s32[4,128]{1,0:T(4,128)} %bitcast.11, f32[2,16,64,128]{3,2,1,0:T(8,128)} %bitcast.10, f32[128,640]{1,0:T(8,128)} %proj_h.1), custom_call_target="tpu_custom_call" | custom-call | flops 335544320 | bytes 3145728 | tf_op jit(solution)/shard_map/pallas_call | solution.py:232
  2.9 30.4 %all_to_all.20 = bf16[128,32,128]{2,1,0:T(8,128)(2,1)S(1)} all-to-all(bf16[128,32,128]{2,1,0:T(8,128)(2,1)S(1)} %get-tuple-element.13), channel_id=1, replica_groups=mesh['row'=16,'col'=8] {'row','col'}, dimensions={0} | all-to-all | bytes 2097152 | tf_op jit(solution)/shard_map/all_to_all | solution.py:217
  33.3 0.7 shard_map.65
  34.0 0.0 copy-start
  34.0 0.0 copy-start.2
  34.0 17.8 %all_to_all.21.got = bf16[128,16,128]{2,1,0:T(8,128)(2,1)S(1)} all-to-all(bf16[128,16,128]{2,1,0:T(8,128)(2,1)S(1)} %bitcast.8), channel_id=1, replica_groups=mesh['row'=16,'col'=8] {'row','col'}, dimensions={0} | all-to-all | bytes 1048576 | tf_op jit(solution)/shard_map/all_to_all | solution.py:217
  51.8 0.0 copy-done
  51.8 0.0 copy-done.2
  51.8 2.1 %shard_map.66 = (bf16[128,32,128]{2,1,0:T(8,128)(2,1)S(1)}, f32[128,2048]{1,0:T(8,128)S(1)}, f32[128,2048]{1,0:T(8,128)S(1)}) custom-call(f32[16,128]{1,0:T(8,128)S(1)} %get-tuple-element.12.mask, bf16[128,16,128]{2,1,0:T(8,128)(2,1)S(1)} %all_to_all.21.got, f32[128,2048]{1,0:T(8,128)S(1)} %get-tuple-element.14.flat, ...), custom_call_target="tpu_custom_call" | custom-call | flops 402653184 | bytes 3145728 | tf_op jit(solution)/shard_map/pallas_call | solution.py:236
  53.9 23.2 %all_to_all.22 = bf16[128,32,128]{2,1,0:T(8,128)(2,1)S(1)} all-to-all(bf16[128,32,128]{2,1,0:T(8,128)(2,1)S(1)} %get-tuple-element.16), channel_id=1, replica_groups=mesh['row'=16,'col'=8] {'row','col'}, dimensions={0} | all-to-all | bytes 2097152 | tf_op jit(solution)/shard_map/all_to_all | solution.py:217
  77.2 0.8 shard_map.67
  78.0 0.0 copy-start.1
  78.0 17.8 %all_to_all.23.got = bf16[128,16,128]{2,1,0:T(8,128)(2,1)S(1)} all-to-all(bf16[128,16,128]{2,1,0:T(8,128)(2,1)S(1)} %bitcast.9), channel_id=1, replica_groups=mesh['row'=16,'col'=8] {'row','col'}, dimensions={0} | all-to-all | bytes 1048576 | tf_op jit(solution)/shard_map/all_to_all | solution.py:217
  95.7 0.0 copy-done.1
  95.7 1.7 %shard_map.68 = f32[32,64,128]{2,1,0:T(8,128)} custom-call(bf16[128,16,128]{2,1,0:T(8,128)(2,1)S(1)} %all_to_all.23.got, f32[128,2048]{1,0:T(8,128)S(1)} %get-tuple-element.17.first, f32[128,2048]{1,0:T(8,128)S(1)} %get-tuple-element.18.gating, f32[128,128]{1,0:T(8,128)S(1)} %copy-done.1), custom_call_target="tpu_custom_call" | custom-call | flops 67108864 | bytes 3145728 | tf_op jit(solution)/shard_map/pallas_call | solution.py:240
Async XLA Ops:
  34.0 17.8 %copy-start = (f32[128,640]{1,0:T(8,128)S(1)}, f32[128,640]{1,0:T(8,128)}, u32[]{:S(2)}) copy-start(f32[128,640]{1,0:T(8,128)} %proj.1) | copy-start | bytes 983044
  34.0 17.8 %copy-start.2 = (f32[128,128]{1,0:T(8,128)S(1)}, f32[128,128]{1,0:T(8,128)}, u32[]{:S(2)}) copy-start(f32[128,128]{1,0:T(8,128)} %final.2) | copy-start | bytes 196612
  78.0 17.8 %copy-start.1 = (f32[128,128]{1,0:T(8,128)S(1)}, f32[128,128]{1,0:T(8,128)}, u32[]{:S(2)}) copy-start(f32[128,128]{1,0:T(8,128)} %final.3) | copy-start | bytes 196612

commit v8 on v7

--- a/solution.py
+++ b/solution.py
@@ -157,9 +157,8 @@
             out[n, 2 * m + 1] = jnp.where(low, turn(top), bottom).astype(BF16)
 
 
-def unpack(got, triangle):
-    for k in range(0, 128, 32):
-        triangle[:, k : k + 32, :] = jnp.swapaxes(got[k : k + 32], 0, 1)
+def unpack(got):
+    return jnp.swapaxes(got[...], 0, 1)
 
 
 def finish(triangle, tile, flat, gating, closing):
@@ -171,11 +170,11 @@
 
 
 def middle_kernel(
-    mask, got, flat, gating, final, proj, out, first, next_gating, held, triangle
+    mask, got, flat, gating, final, proj, out, first, next_gating, held
 ):
     weights = halved(proj)
     closing = halved(final)
-    unpack(got, triangle)
+    triangle = unpack(got)
     for tile in range(0, TILES, 2):
         first[:, 128 * tile : 128 * (tile + 2)] = finish(triangle, tile, flat, gating, closing)
     for tile in range(0, TILES, 2):
@@ -184,9 +183,9 @@
     pack(held, out)
 
 
-def last_kernel(got, first, gating, final, out, triangle, done, semaphores):
+def last_kernel(got, first, gating, final, out, done, semaphores):
     closing = halved(final)
-    unpack(got, triangle)
+    triangle = unpack(got)
     copies = []
     for tile in range(0, TILES, 2):
         values = finish(triangle, tile, first, gating, closing)
@@ -211,7 +210,6 @@
     answer = struct((16, 8, 16, 128), BF16)
     whole = struct((128, 2048), F32)
     held = pltpu.VMEM((2, TILES, 128, 128), F32)
-    sums_held = pltpu.VMEM((TILES, 128, 128), BF16)
 
     def swap(values):
         return lax.all_to_all(values, axes, 0, 0, tiled=True)
@@ -234,7 +232,7 @@
     )(*[pltpu.with_memory_space_constraint(v, pltpu.HBM) for v in (lines, pair.reshape(2, TILES, HALF, 128), out_proj)])
     sums = swap(triangle(swap(sent), 1))
     sent, first, gating = call(
-        middle_kernel, (message, whole, whole), [held, sums_held], [VMEM] * 6, 2 * 2048 * 128 * 768
+        middle_kernel, (message, whole, whole), [held], [VMEM] * 6, 2 * 2048 * 128 * 768
     )(mask, sums, flat, gating, out_final, in_proj)
     sums = swap(triangle(swap(sent), 0))
     return pl.pallas_call(
@@ -242,7 +240,7 @@
         out_shape=struct(pair.shape, F32),
         in_specs=[VMEM] * 4,
         out_specs=HBM,
-        scratch_shapes=[sums_held, pltpu.VMEM(pair.shape, F32), pltpu.SemaphoreType.DMA((8,))],
+        scratch_shapes=[pltpu.VMEM(pair.shape, F32), pltpu.SemaphoreType.DMA((8,))],
         compiler_params=pltpu.CompilerParams(vmem_limit_bytes=16 * 1024 * 1024),
         cost_estimate=pl.CostEstimate(flops=2 * 2048 * 128 * 128, bytes_accessed=3 << 20, transcendentals=0),
     )(sums, first, gating, in_final)

time: 97.7 us -> 97.5 us (level)
  no operation moved by 1% of the time
where the time goes in v8:
time: 97.5 us; the launch traced here: 97.3 us
  blocking collectives  89.2 us (91%)
  Pallas kernels  8.04 us (8%)
    all_to_all x4, blocking collectives, swap(): return lax.all_to_all(values, axes, 0, 0, tiled=True)  89.2 us
    pallas_call x1, Pallas kernels, shards(): call(project_kernel, (message, whole, whole, struct((TILES, 128), F32)),...  2.9 us
    pallas_call x1, Pallas kernels, shards(): call(middle_kernel, (message, whole, whole), [held], [VMEM] * 6, 2 * 2048...  2.04 us

profile of v8, /device:TPU:1, one launch (start us, length us, event | category | flops | bytes accessed | tf_op | source)
XLA Modules:
  0.0 97.3 jit_solution(4659298751588721776)
XLA Ops:
  0.0 2.9 %shard_map.64 = (bf16[128,32,128]{2,1,0:T(8,128)(2,1)S(1)}, f32[128,2048]{1,0:T(8,128)S(1)}, f32[128,2048]{1,0:T(8,128)S(1)}, f32[16,128]{1,0:T(8,128)S(1)}) custom-call(s32[4,128]{1,0:T(4,128)} %bitcast.11, f32[2,16,64,128]{3,2,1,0:T(8,128)} %bitcast.10, f32[128,640]{1,0:T(8,128)} %proj_h.1), custom_call_target="tpu_custom_call" | custom-call | flops 335544320 | bytes 3145728 | tf_op jit(solution)/shard_map/pallas_call | solution.py:230
  2.9 30.4 %all_to_all.20 = bf16[128,32,128]{2,1,0:T(8,128)(2,1)S(1)} all-to-all(bf16[128,32,128]{2,1,0:T(8,128)(2,1)S(1)} %get-tuple-element.13), channel_id=1, replica_groups=mesh['row'=16,'col'=8] {'row','col'}, dimensions={0} | all-to-all | bytes 2097152 | tf_op jit(solution)/shard_map/all_to_all | solution.py:215
  33.3 0.7 shard_map.65
  34.0 0.0 copy-start
  34.0 0.0 copy-start.2
  34.0 17.8 %all_to_all.21.got = bf16[128,16,128]{2,1,0:T(8,128)(2,1)S(1)} all-to-all(bf16[128,16,128]{2,1,0:T(8,128)(2,1)S(1)} %bitcast.8), channel_id=1, replica_groups=mesh['row'=16,'col'=8] {'row','col'}, dimensions={0} | all-to-all | bytes 1048576 | tf_op jit(solution)/shard_map/all_to_all | solution.py:215
  51.8 0.0 copy-done
  51.8 0.0 copy-done.2
  51.8 2.0 %shard_map.66 = (bf16[128,32,128]{2,1,0:T(8,128)(2,1)S(1)}, f32[128,2048]{1,0:T(8,128)S(1)}, f32[128,2048]{1,0:T(8,128)S(1)}) custom-call(f32[16,128]{1,0:T(8,128)S(1)} %get-tuple-element.12.mask, bf16[128,16,128]{2,1,0:T(8,128)(2,1)S(1)} %all_to_all.21.got, f32[128,2048]{1,0:T(8,128)S(1)} %get-tuple-element.14.flat, ...), custom_call_target="tpu_custom_call" | custom-call | flops 402653184 | bytes 3145728 | tf_op jit(solution)/shard_map/pallas_call | solution.py:234
  53.8 23.2 %all_to_all.22 = bf16[128,32,128]{2,1,0:T(8,128)(2,1)S(1)} all-to-all(bf16[128,32,128]{2,1,0:T(8,128)(2,1)S(1)} %get-tuple-element.16), channel_id=1, replica_groups=mesh['row'=16,'col'=8] {'row','col'}, dimensions={0} | all-to-all | bytes 2097152 | tf_op jit(solution)/shard_map/all_to_all | solution.py:215
  77.1 0.8 shard_map.67
  77.9 0.0 copy-start.1
  77.9 17.8 %all_to_all.23.got = bf16[128,16,128]{2,1,0:T(8,128)(2,1)S(1)} all-to-all(bf16[128,16,128]{2,1,0:T(8,128)(2,1)S(1)} %bitcast.9), channel_id=1, replica_groups=mesh['row'=16,'col'=8] {'row','col'}, dimensions={0} | all-to-all | bytes 1048576 | tf_op jit(solution)/shard_map/all_to_all | solution.py:215
  95.6 0.0 copy-done.1
  95.6 1.6 %shard_map.68 = f32[32,64,128]{2,1,0:T(8,128)} custom-call(bf16[128,16,128]{2,1,0:T(8,128)(2,1)S(1)} %all_to_all.23.got, f32[128,2048]{1,0:T(8,128)S(1)} %get-tuple-element.17.first, f32[128,2048]{1,0:T(8,128)S(1)} %get-tuple-element.18.gating, f32[128,128]{1,0:T(8,128)S(1)} %copy-done.1), custom_call_target="tpu_custom_call" | custom-call | flops 67108864 | bytes 3145728 | tf_op jit(solution)/shard_map/pallas_call | solution.py:238
Async XLA Ops:
  34.0 17.8 %copy-start = (f32[128,640]{1,0:T(8,128)S(1)}, f32[128,640]{1,0:T(8,128)}, u32[]{:S(2)}) copy-start(f32[128,640]{1,0:T(8,128)} %proj.1) | copy-start | bytes 983044
  34.0 17.8 %copy-start.2 = (f32[128,128]{1,0:T(8,128)S(1)}, f32[128,128]{1,0:T(8,128)}, u32[]{:S(2)}) copy-start(f32[128,128]{1,0:T(8,128)} %final.2) | copy-start | bytes 196612
  77.9 17.8 %copy-start.1 = (f32[128,128]{1,0:T(8,128)S(1)}, f32[128,128]{1,0:T(8,128)}, u32[]{:S(2)}) copy-start(f32[128,128]{1,0:T(8,128)} %final.3) | copy-start | bytes 196612

commit v9 on v8

--- a/solution.py
+++ b/solution.py
@@ -147,7 +147,10 @@
 
 def triangle_kernel(contract, got, out):
     left, right = operands(got)
-    sums = dot(left, right, ((contract,), (contract,))).reshape(16, 2, 16, 512)
+    sums = dot(left, right, ((contract,), (contract,)))
+    if contract == 1:
+        sums = sums.astype(BF16)
+    sums = sums.reshape(16, 2, 16, 512)
     low = low_lanes((16, 128))
     for n in range(16):
         for m in range(4):

time: 97.5 us -> 97.5 us (level)
  no operation moved by 1% of the time
where the time goes in v9:
time: 97.5 us; the launch traced here: 97.2 us
  blocking collectives  89.2 us (91%)
  Pallas kernels  8.01 us (8%)
    all_to_all x4, blocking collectives, swap(): return lax.all_to_all(values, axes, 0, 0, tiled=True)  89.2 us
    pallas_call x1, Pallas kernels, shards(): call(project_kernel, (message, whole, whole, struct((TILES, 128), F32)),...  2.9 us
    pallas_call x1, Pallas kernels, shards(): call(middle_kernel, (message, whole, whole), [held], [VMEM] * 6, 2 * 2048...  2.04 us

profile of v9, /device:TPU:1, one launch (start us, length us, event | category | flops | bytes accessed | tf_op | source)
XLA Modules:
  0.0 97.2 jit_solution(14938713377580494950)
XLA Ops:
  0.0 2.9 %shard_map.64 = (bf16[128,32,128]{2,1,0:T(8,128)(2,1)S(1)}, f32[128,2048]{1,0:T(8,128)S(1)}, f32[128,2048]{1,0:T(8,128)S(1)}, f32[16,128]{1,0:T(8,128)S(1)}) custom-call(s32[4,128]{1,0:T(4,128)} %bitcast.11, f32[2,16,64,128]{3,2,1,0:T(8,128)} %bitcast.10, f32[128,640]{1,0:T(8,128)} %proj_h.1), custom_call_target="tpu_custom_call" | custom-call | flops 335544320 | bytes 3145728 | tf_op jit(solution)/shard_map/pallas_call | solution.py:233
  2.9 30.4 %all_to_all.20 = bf16[128,32,128]{2,1,0:T(8,128)(2,1)S(1)} all-to-all(bf16[128,32,128]{2,1,0:T(8,128)(2,1)S(1)} %get-tuple-element.13), channel_id=1, replica_groups=mesh['row'=16,'col'=8] {'row','col'}, dimensions={0} | all-to-all | bytes 2097152 | tf_op jit(solution)/shard_map/all_to_all | solution.py:218
  33.3 0.6 shard_map.65
  34.0 0.0 copy-start
  34.0 0.0 copy-start.2
  34.0 17.8 %all_to_all.21.got = bf16[128,16,128]{2,1,0:T(8,128)(2,1)S(1)} all-to-all(bf16[128,16,128]{2,1,0:T(8,128)(2,1)S(1)} %bitcast.8), channel_id=1, replica_groups=mesh['row'=16,'col'=8] {'row','col'}, dimensions={0} | all-to-all | bytes 1048576 | tf_op jit(solution)/shard_map/all_to_all | solution.py:218
  51.8 0.0 copy-done
  51.8 0.0 copy-done.2
  51.8 2.0 %shard_map.66 = (bf16[128,32,128]{2,1,0:T(8,128)(2,1)S(1)}, f32[128,2048]{1,0:T(8,128)S(1)}, f32[128,2048]{1,0:T(8,128)S(1)}) custom-call(f32[16,128]{1,0:T(8,128)S(1)} %get-tuple-element.12.mask, bf16[128,16,128]{2,1,0:T(8,128)(2,1)S(1)} %all_to_all.21.got, f32[128,2048]{1,0:T(8,128)S(1)} %get-tuple-element.14.flat, ...), custom_call_target="tpu_custom_call" | custom-call | flops 402653184 | bytes 3145728 | tf_op jit(solution)/shard_map/pallas_call | solution.py:237
  53.8 23.2 %all_to_all.22 = bf16[128,32,128]{2,1,0:T(8,128)(2,1)S(1)} all-to-all(bf16[128,32,128]{2,1,0:T(8,128)(2,1)S(1)} %get-tuple-element.16), channel_id=1, replica_groups=mesh['row'=16,'col'=8] {'row','col'}, dimensions={0} | all-to-all | bytes 2097152 | tf_op jit(solution)/shard_map/all_to_all | solution.py:218
  77.0 0.8 shard_map.67
  77.8 0.0 copy-start.1
  77.8 17.8 %all_to_all.23.got = bf16[128,16,128]{2,1,0:T(8,128)(2,1)S(1)} all-to-all(bf16[128,16,128]{2,1,0:T(8,128)(2,1)S(1)} %bitcast.9), channel_id=1, replica_groups=mesh['row'=16,'col'=8] {'row','col'}, dimensions={0} | all-to-all | bytes 1048576 | tf_op jit(solution)/shard_map/all_to_all | solution.py:218
  95.6 0.0 copy-done.1
  95.6 1.6 %shard_map.68 = f32[32,64,128]{2,1,0:T(8,128)} custom-call(bf16[128,16,128]{2,1,0:T(8,128)(2,1)S(1)} %all_to_all.23.got, f32[128,2048]{1,0:T(8,128)S(1)} %get-tuple-element.17.first, f32[128,2048]{1,0:T(8,128)S(1)} %get-tuple-element.18.gating, f32[128,128]{1,0:T(8,128)S(1)} %copy-done.1), custom_call_target="tpu_custom_call" | custom-call | flops 67108864 | bytes 3145728 | tf_op jit(solution)/shard_map/pallas_call | solution.py:241
Async XLA Ops:
  34.0 17.8 %copy-start = (f32[128,640]{1,0:T(8,128)S(1)}, f32[128,640]{1,0:T(8,128)}, u32[]{:S(2)}) copy-start(f32[128,640]{1,0:T(8,128)} %proj.1) | copy-start | bytes 983044
  34.0 17.8 %copy-start.2 = (f32[128,128]{1,0:T(8,128)S(1)}, f32[128,128]{1,0:T(8,128)}, u32[]{:S(2)}) copy-start(f32[128,128]{1,0:T(8,128)} %final.2) | copy-start | bytes 196612
  77.8 17.8 %copy-start.1 = (f32[128,128]{1,0:T(8,128)S(1)}, f32[128,128]{1,0:T(8,128)}, u32[]{:S(2)}) copy-start(f32[128,128]{1,0:T(8,128)} %final.3) | copy-start | bytes 196612

commit v10 on v9

--- a/solution.py
+++ b/solution.py
@@ -83,7 +83,7 @@
     return pair[:, tile].reshape(128, 128).T
 
 
-def sides(normed, weights, held, tile):
+def sides(normed, weights, held):
     both = jnp.concatenate(split(normed), axis=0)
 
     def side(k):
@@ -91,7 +91,7 @@
         value = linear[:128] + linear[128:256]
         value = value + jnp.tanh(linear[256:]) * value
         for n in range(2):
-            held[k, tile + n] = value[:, 128 * n : 128 * (n + 1)]
+            held[k].append(value[:, 128 * n : 128 * (n + 1)].astype(BF16))
 
     side(0)
     side(1)
@@ -101,10 +101,10 @@
 def pack(held, out):
     for side in range(2):
         for k in range(0, 128, 32):
-            out[k : k + 32, 16 * side : 16 * side + 16, :] = jnp.swapaxes(held[side, :, k : k + 32, :], 0, 1).astype(BF16)
-
-
-def project_kernel(token_h, pair_h, proj_h, out, flat, gating, mask, held, normed, tokens, pair, proj, semaphores):
+            out[k : k + 32, 16 * side : 16 * side + 16, :] = jnp.swapaxes(jnp.stack([part[k : k + 32] for part in held[side]]), 0, 1)
+
+
+def project_kernel(token_h, pair_h, proj_h, out, flat, gating, mask, normed, tokens, pair, proj, semaphores):
     parts = [(slice(None), pl.ds(4 * k, 4)) for k in range(4)]
     copies = [
         pltpu.make_async_copy(pair_h.at[part], pair.at[part], semaphores.at[k])
@@ -128,9 +128,10 @@
         values = jnp.concatenate([pair_tile(pair, tile), pair_tile(pair, tile + 1)], axis=1)
         flat[:, lanes] = values
         normed[:, lanes] = norm(values, mask_of(mask, tile))
+    held = ([], [])
     for tile in range(0, TILES, 2):
         lanes = slice(128 * tile, 128 * (tile + 2))
-        gating[:, lanes] = sides(normed[:, lanes], weights, held, tile)
+        gating[:, lanes] = sides(normed[:, lanes], weights, held)
     pack(held, out)
 
 
@@ -173,16 +174,17 @@
 
 
 def middle_kernel(
-    mask, got, flat, gating, final, proj, out, first, next_gating, held
+    mask, got, flat, gating, final, proj, out, first, next_gating
 ):
     weights = halved(proj)
     closing = halved(final)
     triangle = unpack(got)
     for tile in range(0, TILES, 2):
         first[:, 128 * tile : 128 * (tile + 2)] = finish(triangle, tile, flat, gating, closing)
+    held = ([], [])
     for tile in range(0, TILES, 2):
         lanes = slice(128 * tile, 128 * (tile + 2))
-        next_gating[:, lanes] = sides(norm(first[:, lanes], mask_of(mask, tile)), weights, held, tile)
+        next_gating[:, lanes] = sides(norm(first[:, lanes], mask_of(mask, tile)), weights, held)
     pack(held, out)
 
 
@@ -212,7 +214,6 @@
     message = struct((128, 32, 128), BF16)
     answer = struct((16, 8, 16, 128), BF16)
     whole = struct((128, 2048), F32)
-    held = pltpu.VMEM((2, TILES, 128, 128), F32)
 
     def swap(values):
         return lax.all_to_all(values, axes, 0, 0, tiled=True)
@@ -223,7 +224,6 @@
         return sums.reshape(128, 16, 128)
 
     scratch = [
-        held,
         pltpu.VMEM((128, 2048), F32),
         pltpu.VMEM((4, 128), jnp.int32),
         pltpu.VMEM((2, TILES, HALF, 128), F32),
@@ -235,7 +235,7 @@
     )(*[pltpu.with_memory_space_constraint(v, pltpu.HBM) for v in (lines, pair.reshape(2, TILES, HALF, 128), out_proj)])
     sums = swap(triangle(swap(sent), 1))
     sent, first, gating = call(
-        middle_kernel, (message, whole, whole), [held], [VMEM] * 6, 2 * 2048 * 128 * 768
+        middle_kernel, (message, whole, whole), [], [VMEM] * 6, 2 * 2048 * 128 * 768
     )(mask, sums, flat, gating, out_final, in_proj)
     sums = swap(triangle(swap(sent), 0))
     return pl.pallas_call(

time: 97.5 us -> 97.5 us (level)
  no operation moved by 1% of the time
where the time goes in v10:
time: 97.5 us; the launch traced here: 97.3 us
  blocking collectives  89.2 us (91%)
  Pallas kernels  8.04 us (8%)
    all_to_all x4, blocking collectives, swap(): return lax.all_to_all(values, axes, 0, 0, tiled=True)  89.2 us
    pallas_call x1, Pallas kernels, shards(): call(project_kernel, (message, whole, whole, struct((TILES, 128), F32)),...  2.91 us
    pallas_call x1, Pallas kernels, shards(): call(middle_kernel, (message, whole, whole), [], [VMEM] * 6, 2 * 2048 * 1...  2.07 us

profile of v10, /device:TPU:1, one launch (start us, length us, event | category | flops | bytes accessed | tf_op | source)
XLA Modules:
  0.0 97.3 jit_solution(1936961249542799717)
XLA Ops:
  0.0 2.9 %shard_map.64 = (bf16[128,32,128]{2,1,0:T(8,128)(2,1)S(1)}, f32[128,2048]{1,0:T(8,128)S(1)}, f32[128,2048]{1,0:T(8,128)S(1)}, f32[16,128]{1,0:T(8,128)S(1)}) custom-call(s32[4,128]{1,0:T(4,128)} %bitcast.11, f32[2,16,64,128]{3,2,1,0:T(8,128)} %bitcast.10, f32[128,640]{1,0:T(8,128)} %proj_h.1), custom_call_target="tpu_custom_call" | custom-call | flops 335544320 | bytes 3145728 | tf_op jit(solution)/shard_map/pallas_call | solution.py:233
  2.9 30.4 %all_to_all.20 = bf16[128,32,128]{2,1,0:T(8,128)(2,1)S(1)} all-to-all(bf16[128,32,128]{2,1,0:T(8,128)(2,1)S(1)} %get-tuple-element.13), channel_id=1, replica_groups=mesh['row'=16,'col'=8] {'row','col'}, dimensions={0} | all-to-all | bytes 2097152 | tf_op jit(solution)/shard_map/all_to_all | solution.py:219
  33.4 0.6 shard_map.65
  34.0 0.0 copy-start
  34.0 0.0 copy-start.2
  34.0 17.8 %all_to_all.21.got = bf16[128,16,128]{2,1,0:T(8,128)(2,1)S(1)} all-to-all(bf16[128,16,128]{2,1,0:T(8,128)(2,1)S(1)} %bitcast.8), channel_id=1, replica_groups=mesh['row'=16,'col'=8] {'row','col'}, dimensions={0} | all-to-all | bytes 1048576 | tf_op jit(solution)/shard_map/all_to_all | solution.py:219
  51.8 0.0 copy-done
  51.8 0.0 copy-done.2
  51.8 2.1 %shard_map.66 = (bf16[128,32,128]{2,1,0:T(8,128)(2,1)S(1)}, f32[128,2048]{1,0:T(8,128)S(1)}, f32[128,2048]{1,0:T(8,128)S(1)}) custom-call(f32[16,128]{1,0:T(8,128)S(1)} %get-tuple-element.12.mask, bf16[128,16,128]{2,1,0:T(8,128)(2,1)S(1)} %all_to_all.21.got, f32[128,2048]{1,0:T(8,128)S(1)} %get-tuple-element.14.flat, ...), custom_call_target="tpu_custom_call" | custom-call | flops 402653184 | bytes 3145728 | tf_op jit(solution)/shard_map/pallas_call | solution.py:237
  53.9 23.2 %all_to_all.22 = bf16[128,32,128]{2,1,0:T(8,128)(2,1)S(1)} all-to-all(bf16[128,32,128]{2,1,0:T(8,128)(2,1)S(1)} %get-tuple-element.16), channel_id=1, replica_groups=mesh['row'=16,'col'=8] {'row','col'}, dimensions={0} | all-to-all | bytes 2097152 | tf_op jit(solution)/shard_map/all_to_all | solution.py:219
  77.1 0.8 shard_map.67
  77.9 0.0 copy-start.1
  77.9 17.8 %all_to_all.23.got = bf16[128,16,128]{2,1,0:T(8,128)(2,1)S(1)} all-to-all(bf16[128,16,128]{2,1,0:T(8,128)(2,1)S(1)} %bitcast.9), channel_id=1, replica_groups=mesh['row'=16,'col'=8] {'row','col'}, dimensions={0} | all-to-all | bytes 1048576 | tf_op jit(solution)/shard_map/all_to_all | solution.py:219
  95.6 0.0 copy-done.1
  95.6 1.6 %shard_map.68 = f32[32,64,128]{2,1,0:T(8,128)} custom-call(bf16[128,16,128]{2,1,0:T(8,128)(2,1)S(1)} %all_to_all.23.got, f32[128,2048]{1,0:T(8,128)S(1)} %get-tuple-element.17.first, f32[128,2048]{1,0:T(8,128)S(1)} %get-tuple-element.18.gating, f32[128,128]{1,0:T(8,128)S(1)} %copy-done.1), custom_call_target="tpu_custom_call" | custom-call | flops 67108864 | bytes 3145728 | tf_op jit(solution)/shard_map/pallas_call | solution.py:241
Async XLA Ops:
  34.0 17.8 %copy-start = (f32[128,640]{1,0:T(8,128)S(1)}, f32[128,640]{1,0:T(8,128)}, u32[]{:S(2)}) copy-start(f32[128,640]{1,0:T(8,128)} %proj.1) | copy-start | bytes 983044
  34.0 17.8 %copy-start.2 = (f32[128,128]{1,0:T(8,128)S(1)}, f32[128,128]{1,0:T(8,128)}, u32[]{:S(2)}) copy-start(f32[128,128]{1,0:T(8,128)} %final.2) | copy-start | bytes 196612
  77.9 17.8 %copy-start.1 = (f32[128,128]{1,0:T(8,128)S(1)}, f32[128,128]{1,0:T(8,128)}, u32[]{:S(2)}) copy-start(f32[128,128]{1,0:T(8,128)} %final.3) | copy-start | bytes 196612
